TPU v7x, 32 devices: a whole 2x2x4 slice. The times are simulated.
32 devices in a mesh: tour: 16 (over z, x, core), feat: 2 (over y).
Axes of the slice: x: 2, y: 2, z: 4, core: 2. Of those that a mesh axis runs over, the one named last changes fastest.
Arguments:
- projected: bfloat16 [8192, 1024], P('tour', 'feat'), may hold values from -220 to 220
- sharpness: float32 [], replicated, may hold values from 5 to 250
- partners: int32 [8, 16], replicated, may hold values from 0 to 15, as said below
- positives: int32 [8192], P('tour'), may hold values from 0 to 8191, as said below
Outputs:
- row_loss: float32 [8192], P('tour')
- view_grad: float32 [8192, 1024], P('tour', 'feat')
Inputs may be any that keep to these rules, and one draw needn't show every extreme that they name: For each round r there is one number m_r with partners[r, a] = a XOR m_r for every block a; m_r = M XOR s_r, where M is a nonzero multiple of 8 and s_0, ..., s_7 is an ordering of 0 to 7. positives pairs the views of each block of 512 views among themselves: positives_i lies in i's block, differs from i, and positives of positives_i is i.
All inputs are finite; a program needn't handle non-finite values.
Results may differ from a plain program's by a relative error of at most 0.008.
Values may be sent and summed in bfloat16 or wider, within the bound.
A program may use at most 128 MiB of HBM per device.

v0:
```python
from functools import reduce

import jax
import jax.numpy as jnp
from jax import lax
from jax.sharding import PartitionSpec as P

EPSILON = 1e-06


def from_partner(value, axis, stride):
    mask = 2**stride
    pairs = [(source, source ^ mask) for source in range(lax.axis_size(axis))]
    return lax.ppermute(value, axis, pairs)


def mask_bit(round_masks, bit_index):
    return jnp.bitwise_and(jnp.right_shift(round_masks, bit_index), 1) == 1


def deliver_each(block, round_masks, bits_count):
    routed = []
    for round_index in range(round_masks.shape[0]):
        moving = block
        for bit_index in range(bits_count):
            arrived = from_partner(moving, "tour", bit_index)
            moving = jnp.where(mask_bit(round_masks[round_index], bit_index), arrived, moving)
        routed.append(moving)
    return routed


def similar(queries, key_block):
    return jnp.einsum("qd,kd->qk", queries, key_block, preferred_element_type=jnp.float32)


def per_device(projected, sharpness, partners, positives):
    bits_count = lax.axis_size("tour").bit_length() - 1
    block_index = lax.axis_index("tour")
    row_count = projected.shape[0]
    round_masks = jnp.bitwise_xor(
        lax.dynamic_index_in_dim(partners, block_index, 1, keepdims=False), block_index
    )
    round_count = round_masks.shape[0]
    low_bits = round_count.bit_length() - 1
    high_mask = jnp.left_shift(jnp.right_shift(round_masks[0], low_bits), low_bits)
    code_masks = jnp.bitwise_xor(high_mask, jnp.arange(round_count, dtype=jnp.int32))
    local_pos = positives - block_index * row_count
    floats = projected.astype(jnp.float32)
    inverse = lax.rsqrt(lax.psum(jnp.sum(floats * floats, -1), "feat") + EPSILON)
    unit_rows = floats * inverse[:, None]
    embedded = unit_rows.astype(jnp.bfloat16)
    partner_blocks = deliver_each(embedded, code_masks, bits_count)

    def scored(key_block):
        return lax.psum(similar(embedded, key_block), "feat") * sharpness

    columns = jnp.arange(row_count, dtype=jnp.int32)[None, :]
    query_ids = jnp.arange(embedded.shape[0], dtype=jnp.int32)[:, None]
    own_scores = jnp.where(columns == query_ids, -jnp.inf, scored(embedded))
    all_scores = [own_scores] + [scored(key_block) for key_block in partner_blocks]
    row_peak = reduce(jnp.maximum, [jnp.max(block_scores, -1) for block_scores in all_scores])
    exp_total = reduce(
        jnp.add,
        [jnp.sum(jnp.exp(block_scores - row_peak[:, None]), -1) for block_scores in all_scores],
    )
    lse_rows = row_peak + jnp.log(exp_total)
    pos_hit = columns == local_pos[:, None]
    loss_rows = lse_rows - jnp.sum(jnp.where(pos_hit, own_scores, 0.0), -1)
    stacked = jnp.broadcast_to(lse_rows[None, :], (round_count, row_count))
    for bit_index in range(bits_count):
        arrived = from_partner(stacked, "tour", bit_index)
        stacked = jnp.where(mask_bit(code_masks, bit_index)[:, None], arrived, stacked)
    own_weight = (
        jnp.exp(own_scores - lse_rows[:, None])
        + jnp.exp(own_scores - lse_rows[None, :])
        - 2.0 * pos_hit.astype(jnp.float32)
    )
    unit_grad = jnp.dot(
        own_weight.astype(jnp.bfloat16), embedded, preferred_element_type=jnp.float32
    )
    for round_index in range(len(partner_blocks)):
        block_scores = all_scores[round_index + 1]
        weight = jnp.exp(block_scores - lse_rows[:, None]) + jnp.exp(
            block_scores - stacked[round_index][None, :]
        )
        unit_grad = unit_grad + jnp.dot(
            weight.astype(jnp.bfloat16),
            partner_blocks[round_index],
            preferred_element_type=jnp.float32,
        )
    unit_grad = unit_grad * sharpness
    radial = lax.psum(jnp.sum(unit_rows * unit_grad, -1), "feat")
    view_grad = inverse[:, None] * (unit_grad - unit_rows * radial[:, None])
    return (loss_rows, view_grad)


def solution(mesh):
    in_specs = (P("tour", "feat"), P(), P(), P("tour"))
    out_specs = (P("tour"), P("tour", "feat"))
    return jax.shard_map(
        per_device, mesh=mesh, in_specs=in_specs, out_specs=out_specs, check_vma=False
    )
```

profile of v0, /device:TPU:0, one launch (start us, length us, event | category | flops | bytes accessed | tf_op | source)
XLA Modules:
  0.0 599.0 jit_solution(14432198386952046044)
XLA Ops:
  8.5 5.9 psum.77
  22.6 2.1 collective-permute-start.1
  41.2 2.0 collective-permute-start.7
  43.2 2.0 collective-permute-start.13
  45.4 9.1 %collective-permute-done.4 = bf16[512,512]{1,0:T(8,128)(2,1)S(1)} collective-permute-done((bf16[512,512]{1,0:T(8,128)(2,1)S(1)}, bf16[512,512]{1,0:T(8,128)(2,1)S(1)}, u32[]{:S(2)}, u32[]{:S(2)}) %collective-permute-start.4) | collective-permute-done | bytes 524320 | tf_op jit(solution)/shard_map/ppermute | solution.py:14
  54.6 11.2 %collective-permute-done.7 = bf16[512,512]{1,0:T(8,128)(2,1)S(1)} collective-permute-done((bf16[512,512]{1,0:T(8,128)(2,1)S(1)}, bf16[512,512]{1,0:T(8,128)(2,1)S(1)}, u32[]{:S(2)}, u32[]{:S(2)}) %collective-permute-start.7) | collective-permute-done | bytes 524320 | tf_op jit(solution)/shard_map/ppermute | solution.py:14
  65.8 11.2 %collective-permute-done.10 = bf16[512,512]{1,0:T(8,128)(2,1)S(1)} collective-permute-done((bf16[512,512]{1,0:T(8,128)(2,1)S(1)}, bf16[512,512]{1,0:T(8,128)(2,1)S(1)}, u32[]{:S(2)}, u32[]{:S(2)}) %collective-permute-start.10) | collective-permute-done | bytes 524320 | tf_op jit(solution)/shard_map/ppermute | solution.py:14
  78.6 9.6 %collective-permute-done.13 = bf16[512,512]{1,0:T(8,128)(2,1)S(1)} collective-permute-done((bf16[512,512]{1,0:T(8,128)(2,1)S(1)}, bf16[512,512]{1,0:T(8,128)(2,1)S(1)}, u32[]{:S(2)}, u32[]{:S(2)}) %collective-permute-start.13) | collective-permute-done | bytes 524320 | tf_op jit(solution)/shard_map/ppermute | solution.py:14
  89.8 9.6 %collective-permute-done.16 = bf16[512,512]{1,0:T(8,128)(2,1)S(1)} collective-permute-done((bf16[512,512]{1,0:T(8,128)(2,1)S(1)}, bf16[512,512]{1,0:T(8,128)(2,1)S(1)}, u32[]{:S(2)}, u32[]{:S(2)}) %collective-permute-start.16) | collective-permute-done | bytes 524320 | tf_op jit(solution)/shard_map/ppermute | solution.py:14
  101.1 9.6 %collective-permute-done.19 = bf16[512,512]{1,0:T(8,128)(2,1)S(1)} collective-permute-done((bf16[512,512]{1,0:T(8,128)(2,1)S(1)}, bf16[512,512]{1,0:T(8,128)(2,1)S(1)}, u32[]{:S(2)}, u32[]{:S(2)}) %collective-permute-start.19) | collective-permute-done | bytes 524320 | tf_op jit(solution)/shard_map/ppermute | solution.py:14
  112.3 8.9 %collective-permute-done.22 = bf16[512,512]{1,0:T(8,128)(2,1)S(1)} collective-permute-done((bf16[512,512]{1,0:T(8,128)(2,1)S(1)}, bf16[512,512]{1,0:T(8,128)(2,1)S(1)}, u32[]{:S(2)}, u32[]{:S(2)}) %collective-permute-start.22) | collective-permute-done | bytes 524320 | tf_op jit(solution)/shard_map/ppermute | solution.py:14
  123.4 1.6 collective-permute-start.20
  125.7 2.7 collective-permute-start.3
  128.5 18.8 %collective-permute-done.14 = bf16[512,512]{1,0:T(8,128)(2,1)S(1)} collective-permute-done((bf16[512,512]{1,0:T(8,128)(2,1)S(1)}, bf16[512,512]{1,0:T(8,128)(2,1)S(1)}, u32[]{:S(2)}, u32[]{:S(2)}) %collective-permute-start.14) | collective-permute-done | bytes 524320 | tf_op jit(solution)/shard_map/ppermute | solution.py:14
  147.3 1.7 collective-permute-start.6
  149.0 20.7 %collective-permute-done.17 = bf16[512,512]{1,0:T(8,128)(2,1)S(1)} collective-permute-done((bf16[512,512]{1,0:T(8,128)(2,1)S(1)}, bf16[512,512]{1,0:T(8,128)(2,1)S(1)}, u32[]{:S(2)}, u32[]{:S(2)}) %collective-permute-start.17) | collective-permute-done | bytes 524320 | tf_op jit(solution)/shard_map/ppermute | solution.py:14
  169.8 1.7 collective-permute-start.9
  171.5 10.4 %collective-permute-done.20 = bf16[512,512]{1,0:T(8,128)(2,1)S(1)} collective-permute-done((bf16[512,512]{1,0:T(8,128)(2,1)S(1)}, bf16[512,512]{1,0:T(8,128)(2,1)S(1)}, u32[]{:S(2)}, u32[]{:S(2)}) %collective-permute-start.20) | collective-permute-done | bytes 524320 | tf_op jit(solution)/shard_map/ppermute | solution.py:14
  182.8 8.7 %collective-permute-done.23 = bf16[512,512]{1,0:T(8,128)(2,1)S(1)} collective-permute-done((bf16[512,512]{1,0:T(8,128)(2,1)S(1)}, bf16[512,512]{1,0:T(8,128)(2,1)S(1)}, u32[]{:S(2)}, u32[]{:S(2)}) %collective-permute-start.23) | collective-permute-done | bytes 524320 | tf_op jit(solution)/shard_map/ppermute | solution.py:14
  192.5 2.2 collective-permute-start.18
  198.4 61.8 %collective-permute-done.9 = bf16[512,512]{1,0:T(8,128)(2,1)S(1)} collective-permute-done((bf16[512,512]{1,0:T(8,128)(2,1)S(1)}, bf16[512,512]{1,0:T(8,128)(2,1)S(1)}, u32[]{:S(2)}, u32[]{:S(2)}) %collective-permute-start.9) | collective-permute-done | bytes 524320 | tf_op jit(solution)/shard_map/ppermute | solution.py:14
  261.7 21.0 %collective-permute-done.12 = bf16[512,512]{1,0:T(8,128)(2,1)S(1)} collective-permute-done((bf16[512,512]{1,0:T(8,128)(2,1)S(1)}, bf16[512,512]{1,0:T(8,128)(2,1)S(1)}, u32[]{:S(2)}, u32[]{:S(2)}) %collective-permute-start.12) | collective-permute-done | bytes 524320 | tf_op jit(solution)/shard_map/ppermute | solution.py:14
  284.1 9.8 %collective-permute-done.15 = bf16[512,512]{1,0:T(8,128)(2,1)S(1)} collective-permute-done((bf16[512,512]{1,0:T(8,128)(2,1)S(1)}, bf16[512,512]{1,0:T(8,128)(2,1)S(1)}, u32[]{:S(2)}, u32[]{:S(2)}) %collective-permute-start.15) | collective-permute-done | bytes 524320 | tf_op jit(solution)/shard_map/ppermute | solution.py:14
  295.4 9.7 %collective-permute-done.18 = bf16[512,512]{1,0:T(8,128)(2,1)S(1)} collective-permute-done((bf16[512,512]{1,0:T(8,128)(2,1)S(1)}, bf16[512,512]{1,0:T(8,128)(2,1)S(1)}, u32[]{:S(2)}, u32[]{:S(2)}) %collective-permute-start.18) | collective-permute-done | bytes 524320 | tf_op jit(solution)/shard_map/ppermute | solution.py:14
  306.6 9.7 %collective-permute-done.21 = bf16[512,512]{1,0:T(8,128)(2,1)S(1)} collective-permute-done((bf16[512,512]{1,0:T(8,128)(2,1)S(1)}, bf16[512,512]{1,0:T(8,128)(2,1)S(1)}, u32[]{:S(2)}, u32[]{:S(2)}) %collective-permute-start.21) | collective-permute-done | bytes 524320 | tf_op jit(solution)/shard_map/ppermute | solution.py:14
  317.9 8.7 %collective-permute-done.24 = bf16[512,512]{1,0:T(8,128)(2,1)S(1)} collective-permute-done((bf16[512,512]{1,0:T(8,128)(2,1)S(1)}, bf16[512,512]{1,0:T(8,128)(2,1)S(1)}, u32[]{:S(2)}, u32[]{:S(2)}) %collective-permute-start.24) | collective-permute-done | bytes 524320 | tf_op jit(solution)/shard_map/ppermute | solution.py:14
  330.2 222.6 %all-reduce.3.cloned.1.call-done = (f32[512,512]{1,0:T(8,128)}, f32[512,512]{1,0:T(8,128)}, f32[512,512]{1,0:T(8,128)}, f32[512,512]{1,0:T(8,128)}, f32[512,512]...) async-done(((f32[512,512]{1,0:T(8,128)}, f32[512,512]{1,0:T(8,128)}, f32[512,512]{1,0:T(8,128)}, ...) | async-done | bytes 9437200 | tf_op jit(solution)/shard_map/psum | solution.py:55
  560.8 2.2 select_reduce_fusion
  566.4 2.3 collective-permute-done.26
  570.2 2.2 collective-permute-done.27
  572.5 2.4 collective-permute-start.28
  586.0 4.9 psum.87
  (169 shorter events, 56.4 us)
Async XLA Ops:
  7.2 545.6 %all-reduce.3.cloned.1.call-start = ((), (), s32[]{:S(2)}) async-start(), calls=%async_computation | async-start | bytes 18874368 | tf_op jit(solution)/shard_map/psum | solution.py:55
  14.5 7.7 %collective-permute-start = (bf16[512,512]{1,0:T(8,128)(2,1)S(1)}, bf16[512,512]{1,0:T(8,128)(2,1)S(1)}, u32[]{:S(2)}, u32[]{:S(2)}) collective-permute-start(bf16[512,512]{1,0:T(8,128)(2,1)S(1)} %fusion.9), channel_id=1, source_target_pairs={{0,2},{2,0},{4,6},{6,4},{8,10},{10,8},{12,14},{14,12},{16,18},{18,... | collective-permute-start | bytes 1572872 | tf_op jit(solution)/shard_map/ppermute | solution.py:14
  22.6 22.6 %collective-permute-start.1 = (bf16[512,512]{1,0:T(8,128)(2,1)S(1)}, bf16[512,512]{1,0:T(8,128)(2,1)S(1)}, u32[]{:S(2)}, u32[]{:S(2)}) collective-permute-start(bf16[512,512]{1,0:T(8,128)(2,1)S(1)} %get-tuple-element.23), channel_id=1, source_target_pairs={{0,4},{2,6},{4,0},{6,2},{8,12},{10,14},{12,8},{14,10},{16,20},{18,... | collective-permute-start | bytes 1572872 | tf_op jit(solution)/shard_map/ppermute | solution.py:14
  39.7 14.8 %collective-permute-start.4 = (bf16[512,512]{1,0:T(8,128)(2,1)S(1)}, bf16[512,512]{1,0:T(8,128)(2,1)S(1)}, u32[]{:S(2)}, u32[]{:S(2)}) collective-permute-start(bf16[512,512]{1,0:T(8,128)(2,1)S(1)} %get-tuple-element.30), channel_id=1, source_target_pairs={{0,4},{2,6},{4,0},{6,2},{8,12},{10,14},{12,8},{14,10},{16,20},{18,... | collective-permute-start | bytes 1572872 | tf_op jit(solution)/shard_map/ppermute | solution.py:14
  41.2 24.5 %collective-permute-start.7 = (bf16[512,512]{1,0:T(8,128)(2,1)S(1)}, bf16[512,512]{1,0:T(8,128)(2,1)S(1)}, u32[]{:S(2)}, u32[]{:S(2)}) collective-permute-start(bf16[512,512]{1,0:T(8,128)(2,1)S(1)} %get-tuple-element.29), channel_id=1, source_target_pairs={{0,4},{2,6},{4,0},{6,2},{8,12},{10,14},{12,8},{14,10},{16,20},{18,... | collective-permute-start | bytes 1572872 | tf_op jit(solution)/shard_map/ppermute | solution.py:14
  43.2 33.8 %collective-permute-start.10 = (bf16[512,512]{1,0:T(8,128)(2,1)S(1)}, bf16[512,512]{1,0:T(8,128)(2,1)S(1)}, u32[]{:S(2)}, u32[]{:S(2)}) collective-permute-start(bf16[512,512]{1,0:T(8,128)(2,1)S(1)} %get-tuple-element.28), channel_id=1, source_target_pairs={{0,4},{2,6},{4,0},{6,2},{8,12},{10,14},{12,8},{14,10},{16,20},{18,... | collective-permute-start | bytes 1572872 | tf_op jit(solution)/shard_map/ppermute | solution.py:14
  43.2 45.0 %collective-permute-start.13 = (bf16[512,512]{1,0:T(8,128)(2,1)S(1)}, bf16[512,512]{1,0:T(8,128)(2,1)S(1)}, u32[]{:S(2)}, u32[]{:S(2)}) collective-permute-start(bf16[512,512]{1,0:T(8,128)(2,1)S(1)} %get-tuple-element.27), channel_id=1, source_target_pairs={{0,4},{2,6},{4,0},{6,2},{8,12},{10,14},{12,8},{14,10},{16,20},{18,... | collective-permute-start | bytes 1572872 | tf_op jit(solution)/shard_map/ppermute | solution.py:14
  45.2 54.2 %collective-permute-start.16 = (bf16[512,512]{1,0:T(8,128)(2,1)S(1)}, bf16[512,512]{1,0:T(8,128)(2,1)S(1)}, u32[]{:S(2)}, u32[]{:S(2)}) collective-permute-start(bf16[512,512]{1,0:T(8,128)(2,1)S(1)} %get-tuple-element.26), channel_id=1, source_target_pairs={{0,4},{2,6},{4,0},{6,2},{8,12},{10,14},{12,8},{14,10},{16,20},{18,... | collective-permute-start | bytes 1572872 | tf_op jit(solution)/shard_map/ppermute | solution.py:14
  54.5 56.2 %collective-permute-start.19 = (bf16[512,512]{1,0:T(8,128)(2,1)S(1)}, bf16[512,512]{1,0:T(8,128)(2,1)S(1)}, u32[]{:S(2)}, u32[]{:S(2)}) collective-permute-start(bf16[512,512]{1,0:T(8,128)(2,1)S(1)} %get-tuple-element.25), channel_id=1, source_target_pairs={{0,4},{2,6},{4,0},{6,2},{8,12},{10,14},{12,8},{14,10},{16,20},{18,... | collective-permute-start | bytes 1572872 | tf_op jit(solution)/shard_map/ppermute | solution.py:14
  65.7 55.5 %collective-permute-start.22 = (bf16[512,512]{1,0:T(8,128)(2,1)S(1)}, bf16[512,512]{1,0:T(8,128)(2,1)S(1)}, u32[]{:S(2)}, u32[]{:S(2)}) collective-permute-start(bf16[512,512]{1,0:T(8,128)(2,1)S(1)} %get-tuple-element.24), channel_id=1, source_target_pairs={{0,4},{2,6},{4,0},{6,2},{8,12},{10,14},{12,8},{14,10},{16,20},{18,... | collective-permute-start | bytes 1572872 | tf_op jit(solution)/shard_map/ppermute | solution.py:14
  77.0 45.9 %collective-permute-start.2 = (bf16[512,512]{1,0:T(8,128)(2,1)S(1)}, bf16[512,512]{1,0:T(8,128)(2,1)S(1)}, u32[]{:S(2)}, u32[]{:S(2)}) collective-permute-start(bf16[512,512]{1,0:T(8,128)(2,1)S(1)} %broadcast_select_fusion.29), channel_id=1, source_target_pairs={{0,8},{2,10},{4,12},{6,14},{8,0},{10,2},{12,4},{14,6},{16,24},{18,... | collective-permute-start | bytes 1572872 | tf_op jit(solution)/shard_map/ppermute | solution.py:14
  88.2 35.2 %collective-permute-start.5 = (bf16[512,512]{1,0:T(8,128)(2,1)S(1)}, bf16[512,512]{1,0:T(8,128)(2,1)S(1)}, u32[]{:S(2)}, u32[]{:S(2)}) collective-permute-start(bf16[512,512]{1,0:T(8,128)(2,1)S(1)} %broadcast_select_fusion.25), channel_id=1, source_target_pairs={{0,8},{2,10},{4,12},{6,14},{8,0},{10,2},{12,4},{14,6},{16,24},{18,... | collective-permute-start | bytes 1572872 | tf_op jit(solution)/shard_map/ppermute | solution.py:14
  99.4 25.7 %collective-permute-start.8 = (bf16[512,512]{1,0:T(8,128)(2,1)S(1)}, bf16[512,512]{1,0:T(8,128)(2,1)S(1)}, u32[]{:S(2)}, u32[]{:S(2)}) collective-permute-start(bf16[512,512]{1,0:T(8,128)(2,1)S(1)} %broadcast_select_fusion.21), channel_id=1, source_target_pairs={{0,8},{2,10},{4,12},{6,14},{8,0},{10,2},{12,4},{14,6},{16,24},{18,... | collective-permute-start | bytes 1572872 | tf_op jit(solution)/shard_map/ppermute | solution.py:14
  110.7 15.0 %collective-permute-start.11 = (bf16[512,512]{1,0:T(8,128)(2,1)S(1)}, bf16[512,512]{1,0:T(8,128)(2,1)S(1)}, u32[]{:S(2)}, u32[]{:S(2)}) collective-permute-start(bf16[512,512]{1,0:T(8,128)(2,1)S(1)} %broadcast_select_fusion.17), channel_id=1, source_target_pairs={{0,8},{2,10},{4,12},{6,14},{8,0},{10,2},{12,4},{14,6},{16,24},{18,... | collective-permute-start | bytes 1572872 | tf_op jit(solution)/shard_map/ppermute | solution.py:14
  121.2 26.1 %collective-permute-start.14 = (bf16[512,512]{1,0:T(8,128)(2,1)S(1)}, bf16[512,512]{1,0:T(8,128)(2,1)S(1)}, u32[]{:S(2)}, u32[]{:S(2)}) collective-permute-start(bf16[512,512]{1,0:T(8,128)(2,1)S(1)} %broadcast_select_fusion.13), channel_id=1, source_target_pairs={{0,8},{2,10},{4,12},{6,14},{8,0},{10,2},{12,4},{14,6},{16,24},{18,... | collective-permute-start | bytes 1572872 | tf_op jit(solution)/shard_map/ppermute | solution.py:14
  122.8 46.9 %collective-permute-start.17 = (bf16[512,512]{1,0:T(8,128)(2,1)S(1)}, bf16[512,512]{1,0:T(8,128)(2,1)S(1)}, u32[]{:S(2)}, u32[]{:S(2)}) collective-permute-start(bf16[512,512]{1,0:T(8,128)(2,1)S(1)} %broadcast_select_fusion.9), channel_id=1, source_target_pairs={{0,8},{2,10},{4,12},{6,14},{8,0},{10,2},{12,4},{14,6},{16,24},{18,... | collective-permute-start | bytes 1572872 | tf_op jit(solution)/shard_map/ppermute | solution.py:14
  123.4 58.5 %collective-permute-start.20 = (bf16[512,512]{1,0:T(8,128)(2,1)S(1)}, bf16[512,512]{1,0:T(8,128)(2,1)S(1)}, u32[]{:S(2)}, u32[]{:S(2)}) collective-permute-start(bf16[512,512]{1,0:T(8,128)(2,1)S(1)} %broadcast_select_fusion.5), channel_id=1, source_target_pairs={{0,8},{2,10},{4,12},{6,14},{8,0},{10,2},{12,4},{14,6},{16,24},{18,... | collective-permute-start | bytes 1572872 | tf_op jit(solution)/shard_map/ppermute | solution.py:14
  125.1 66.4 %collective-permute-start.23 = (bf16[512,512]{1,0:T(8,128)(2,1)S(1)}, bf16[512,512]{1,0:T(8,128)(2,1)S(1)}, u32[]{:S(2)}, u32[]{:S(2)}) collective-permute-start(bf16[512,512]{1,0:T(8,128)(2,1)S(1)} %broadcast_select_fusion.1), channel_id=1, source_target_pairs={{0,8},{2,10},{4,12},{6,14},{8,0},{10,2},{12,4},{14,6},{16,24},{18,... | collective-permute-start | bytes 1572872 | tf_op jit(solution)/shard_map/ppermute | solution.py:14
  125.7 66.7 %collective-permute-start.3 = (bf16[512,512]{1,0:T(8,128)(2,1)S(1)}, bf16[512,512]{1,0:T(8,128)(2,1)S(1)}, u32[]{:S(2)}, u32[]{:S(2)}) collective-permute-start(bf16[512,512]{1,0:T(8,128)(2,1)S(1)} %broadcast_select_fusion.30), channel_id=1, source_target_pairs={{0,16},{2,18},{4,20},{6,22},{8,24},{10,26},{12,28},{14,30},{16,0},... | collective-permute-start | bytes 1572872 | tf_op jit(solution)/shard_map/ppermute | solution.py:14
  128.4 154.2 %copy-start.12 = (bf16[512,512]{1,0:T(8,128)(2,1)}, bf16[512,512]{1,0:T(8,128)(2,1)S(1)}, u32[]{:S(2)}) copy-start(bf16[512,512]{1,0:T(8,128)(2,1)S(1)} %broadcast_select_fusion.18) | copy-start | bytes 1572868
  147.3 48.8 %collective-permute-start.6 = (bf16[512,512]{1,0:T(8,128)(2,1)S(1)}, bf16[512,512]{1,0:T(8,128)(2,1)S(1)}, u32[]{:S(2)}, u32[]{:S(2)}) collective-permute-start(bf16[512,512]{1,0:T(8,128)(2,1)S(1)} %broadcast_select_fusion.26), channel_id=1, source_target_pairs={{0,16},{2,18},{4,20},{6,22},{8,24},{10,26},{12,28},{14,30},{16,0},... | collective-permute-start | bytes 1572872 | tf_op jit(solution)/shard_map/ppermute | solution.py:14
  149.0 144.9 %copy-start.14 = (bf16[512,512]{1,0:T(8,128)(2,1)}, bf16[512,512]{1,0:T(8,128)(2,1)S(1)}, u32[]{:S(2)}) copy-start(bf16[512,512]{1,0:T(8,128)(2,1)S(1)} %broadcast_select_fusion.14) | copy-start | bytes 1572868
  169.8 90.4 %collective-permute-start.9 = (bf16[512,512]{1,0:T(8,128)(2,1)S(1)}, bf16[512,512]{1,0:T(8,128)(2,1)S(1)}, u32[]{:S(2)}, u32[]{:S(2)}) collective-permute-start(bf16[512,512]{1,0:T(8,128)(2,1)S(1)} %broadcast_select_fusion.22), channel_id=1, source_target_pairs={{0,16},{2,18},{4,20},{6,22},{8,24},{10,26},{12,28},{14,30},{16,0},... | collective-permute-start | bytes 1572872 | tf_op jit(solution)/shard_map/ppermute | solution.py:14
  181.9 100.7 %collective-permute-start.12 = (bf16[512,512]{1,0:T(8,128)(2,1)S(1)}, bf16[512,512]{1,0:T(8,128)(2,1)S(1)}, u32[]{:S(2)}, u32[]{:S(2)}) collective-permute-start(bf16[512,512]{1,0:T(8,128)(2,1)S(1)} %broadcast_select_fusion.18), channel_id=1, source_target_pairs={{0,16},{2,18},{4,20},{6,22},{8,24},{10,26},{12,28},{14,30},{16,0},... | collective-permute-start | bytes 1572872 | tf_op jit(solution)/shard_map/ppermute | solution.py:14
  191.5 102.4 %collective-permute-start.15 = (bf16[512,512]{1,0:T(8,128)(2,1)S(1)}, bf16[512,512]{1,0:T(8,128)(2,1)S(1)}, u32[]{:S(2)}, u32[]{:S(2)}) collective-permute-start(bf16[512,512]{1,0:T(8,128)(2,1)S(1)} %broadcast_select_fusion.14), channel_id=1, source_target_pairs={{0,16},{2,18},{4,20},{6,22},{8,24},{10,26},{12,28},{14,30},{16,0},... | collective-permute-start | bytes 1572872 | tf_op jit(solution)/shard_map/ppermute | solution.py:14
  192.5 112.7 %collective-permute-start.18 = (bf16[512,512]{1,0:T(8,128)(2,1)S(1)}, bf16[512,512]{1,0:T(8,128)(2,1)S(1)}, u32[]{:S(2)}, u32[]{:S(2)}) collective-permute-start(bf16[512,512]{1,0:T(8,128)(2,1)S(1)} %broadcast_select_fusion.10), channel_id=1, source_target_pairs={{0,16},{2,18},{4,20},{6,22},{8,24},{10,26},{12,28},{14,30},{16,0},... | collective-permute-start | bytes 1572872 | tf_op jit(solution)/shard_map/ppermute | solution.py:14
  196.1 120.3 %collective-permute-start.21 = (bf16[512,512]{1,0:T(8,128)(2,1)S(1)}, bf16[512,512]{1,0:T(8,128)(2,1)S(1)}, u32[]{:S(2)}, u32[]{:S(2)}) collective-permute-start(bf16[512,512]{1,0:T(8,128)(2,1)S(1)} %broadcast_select_fusion.6), channel_id=1, source_target_pairs={{0,16},{2,18},{4,20},{6,22},{8,24},{10,26},{12,28},{14,30},{16,0},... | collective-permute-start | bytes 1572872 | tf_op jit(solution)/shard_map/ppermute | solution.py:14
  260.2 66.4 %collective-permute-start.24 = (bf16[512,512]{1,0:T(8,128)(2,1)S(1)}, bf16[512,512]{1,0:T(8,128)(2,1)S(1)}, u32[]{:S(2)}, u32[]{:S(2)}) collective-permute-start(bf16[512,512]{1,0:T(8,128)(2,1)S(1)} %broadcast_select_fusion.2), channel_id=1, source_target_pairs={{0,16},{2,18},{4,20},{6,22},{8,24},{10,26},{12,28},{14,30},{16,0},... | collective-permute-start | bytes 1572872 | tf_op jit(solution)/shard_map/ppermute | solution.py:14
  563.6 1.2 collective-permute-start.25
  564.9 3.7 collective-permute-start.26
  568.7 3.7 collective-permute-start.27
  572.5 4.6 collective-permute-start.28
  (36 other events, 591.3 us)
Sparse Core Ops, SparseCore 0:
  329.0 223.7 all-reduce.2
where the time goes:
time: 600 us; the launch traced here: 599 us
  waiting for transfers between devices  478 us (80%)
  between operations  35.7 us (6%)
  starting transfers between devices  33 us (6%)
  matrix products  19 us (3%)
  local copies, waits for them, and re-layouts  11.2 us (2%)
  other arithmetic  11 us (2%)
  blocking collectives  10.8 us (2%)
    ppermute x29, waiting for transfers between devices, from_partner(): return lax.ppermute(value, axis, pairs)  256 us
    psum x1, waiting for transfers between devices, scored(): return lax.psum(similar(embedded, key_block), 'feat') * sharpness  223 us
    ppermute x29, starting transfers between devices, from_partner(): return lax.ppermute(value, axis, pairs)  32.9 us
    dot_general x9, matrix products, similar(): jnp.einsum('qd,kd->qk', queries, key_block, preferred_element_type=jnp.fl...  13.3 us
  transfers between devices with their start and end apart: 30, of which 22 were waited for; matrix products, arithmetic and copies ran while one was open for 2% of the time, Pallas kernels for 0%

commit v1 on v0

--- a/solution.py
+++ b/solution.py
@@ -1,8 +1,12 @@
+import functools
+import math
 from functools import reduce
 
 import jax
 import jax.numpy as jnp
 from jax import lax
+from jax.experimental import pallas as pl
+from jax.experimental.pallas import tpu as pltpu
 from jax.sharding import PartitionSpec as P
 
 EPSILON = 1e-06
@@ -33,7 +37,7 @@
     return jnp.einsum("qd,kd->qk", queries, key_block, preferred_element_type=jnp.float32)
 
 
-def per_device(projected, sharpness, partners, positives):
+def per_device_any(projected, sharpness, partners, positives):
     bits_count = lax.axis_size("tour").bit_length() - 1
     block_index = lax.axis_index("tour")
     row_count = projected.shape[0]
@@ -94,6 +98,351 @@
     return (loss_rows, view_grad)
 
 
+MESH = pl.DeviceIdType.MESH
+LOG2E = math.log2(math.e)
+LN2 = math.log(2.0)
+GROUP = 8
+CHUNKS = 8
+FAR = -1e30
+
+
+def flipped(index, mask):
+    bit = 1
+    while bit <= mask:
+        if mask & bit:
+            index = index + bit * (1 - 2 * ((index // bit) % 2))
+        bit *= 2
+    return index
+
+
+def log2_add(a, b):
+    return jnp.maximum(a, b) + LOG2E * jnp.log(1.0 + jnp.exp2(-jnp.abs(a - b)))
+
+
+def dot_nt(a, b):
+    return lax.dot_general(a, b, (((1,), (1,)), ((), ())), preferred_element_type=jnp.float32)
+
+
+def dot_tn(a, b):
+    return lax.dot_general(a, b, (((0,), (0,)), ((), ())), preferred_element_type=jnp.float32)
+
+
+def kernel(
+    mask, rows, width, sharp_ref, proj_ref, pos_ref, loss_ref, grad_ref,
+    raw, q, inv, kb, st, wt, peak, total, spos, lse_own, ex, ex_in, rl, lse_rows, lse_keys,
+    g_out, g_in, rad, rad_out, rad_in,
+    y_send, y_recv, k_send, k_recv, l_send, l_recv, e_send, e_recv, g_send, g_recv, r_send, r_recv,
+):
+    half = rows // 2
+    step_rows = half // CHUNKS
+    t = lax.axis_index("tour")
+    f = lax.axis_index("feat")
+    other = 1 - f
+    peer = (t, other)
+    near = {bit: (flipped(t, bit), f) for bit in (1, 2, 4)}
+    far = [flipped(t, mask ^ j) for j in range(GROUP)]
+    scale = sharp_ref[0, 0] * LOG2E
+
+    barrier = pltpu.get_barrier_semaphore()
+    everyone = [peer] + list(near.values()) + [(d, s) for d in far for s in (f, other)]
+    for device in everyone:
+        pl.semaphore_signal(barrier, inc=1, device_id=device, device_id_type=MESH)
+    pl.semaphore_wait(barrier, len(everyone))
+
+    def remote(src, dst, send, recv, device):
+        return pltpu.make_async_remote_copy(
+            src_ref=src, dst_ref=dst, send_sem=send, recv_sem=recv,
+            device_id=device, device_id_type=MESH,
+        )
+
+    pieces = 4
+    piece = half // pieces
+
+    def y_copy(i):
+        if i < pieces:
+            spot = pl.ds(pl.multiple_of(other * half + i * piece, piece), piece)
+        else:
+            spot = pl.ds(pl.multiple_of(f * half, half), half)
+        return remote(proj_ref.at[spot], raw.at[f, spot], y_send.at[i], y_recv.at[i], peer)
+
+    for i in range(pieces + 1):
+        y_copy(i).start()
+    raw[f] = proj_ref[...]
+
+    def normalise(start, count):
+        spot = pl.ds(start, count)
+        left = raw[0, spot, :].astype(jnp.float32)
+        right = raw[1, spot, :].astype(jnp.float32)
+        squares = jnp.sum(left * left, -1, keepdims=True) + jnp.sum(right * right, -1, keepdims=True)
+        inverse = lax.rsqrt(squares + EPSILON)
+        q[0, spot, :] = (left * inverse).astype(jnp.bfloat16)
+        q[1, spot, :] = (right * inverse).astype(jnp.bfloat16)
+        inv[spot, :] = jnp.broadcast_to(inverse, (count, 128))
+
+    def cross(c):
+        spot = pl.ds(pl.multiple_of(f * half + c * step_rows, step_rows), step_rows)
+        return remote(q.at[:, spot], kb.at[:, c, 0], k_send.at[0, c], k_recv.at[0, c], (far[0], f))
+
+    def forward(src, dst, bit, c):
+        return remote(
+            kb.at[:, c, src], kb.at[:, c, dst], k_send.at[dst, c], k_recv.at[dst, c], near[bit]
+        )
+
+    hops = {1: (0, 1), 2: (0, 2), 3: (2, 1), 4: (0, 4), 5: (4, 1), 6: (4, 2), 7: (6, 1)}
+
+    def send_key(slot, c):
+        if slot == 0:
+            return cross(c)
+        src, bit = hops[slot]
+        return forward(src, slot, bit, c)
+
+    for i in range(pieces):
+        y_copy(i).wait_recv()
+        normalise(pl.multiple_of(f * half + i * piece, piece), piece)
+        for c in range(i * CHUNKS // pieces, (i + 1) * CHUNKS // pieces):
+            cross(c).start()
+
+    tile = 128
+
+    def score(c, keys, own):
+        for part in range(rows // 256):
+            lanes = slice(part * 256, part * 256 + 256)
+            block = (dot_nt(keys(0), q[0, lanes, :]) + dot_nt(keys(1), q[1, lanes, :])) * scale
+            if own:
+                key_ids = lax.broadcasted_iota(jnp.int32, block.shape, 0) + f * half
+                query_ids = lax.broadcasted_iota(jnp.int32, block.shape, 1) + part * 256
+                block = jnp.where(key_ids == query_ids, FAR, block)
+                hit = key_ids == pos_ref[:, lanes]
+                spos[:, lanes] = jnp.sum(jnp.where(hit, block, 0.0), 0, keepdims=True)
+            for i in range(256 // tile):
+                st[part * (256 // tile) + i, c] = block[:, i * tile : (i + 1) * tile]
+            folded = block.reshape(half // 8, 8, 256)
+            top = jnp.max(folded, 0)
+            if own:
+                peak[:, lanes] = top
+                total[:, lanes] = jnp.sum(jnp.exp2(folded - top[None]), 0)
+            else:
+                old = peak[:, lanes]
+                top = jnp.maximum(top, old)
+                peak[:, lanes] = top
+                total[:, lanes] = total[:, lanes] * jnp.exp2(old - top) + jnp.sum(
+                    jnp.exp2(folded - top[None]), 0
+                )
+
+    def own_keys(h):
+        return q[h, pl.ds(pl.multiple_of(f * half, half), half), :]
+
+    def chunk_keys(c):
+        return lambda h: kb[h, c].reshape(half, width)
+
+    def tick(n):
+        @pl.when(n < CHUNKS)
+        def _():
+            send_key(0, n).wait_recv()
+            for slot in (4, 2, 1):
+                send_key(slot, n).start()
+
+        @pl.when((n >= 1) & (n < CHUNKS + 1))
+        def _():
+            send_key(4, n - 1).wait_recv()
+            send_key(6, n - 1).start()
+            send_key(5, n - 1).start()
+            send_key(2, n - 1).wait_recv()
+            send_key(3, n - 1).start()
+
+        @pl.when((n >= 2) & (n < CHUNKS + 2))
+        def _():
+            send_key(6, n - 2).wait_recv()
+            send_key(7, n - 2).start()
+
+        @pl.when(n >= 3)
+        def _():
+            for slot in (1, 3, 5, 7):
+                send_key(slot, n - 3).wait_recv()
+            score(n - 3, chunk_keys(n - 3), False)
+
+    def tick_body(n, carry):
+        tick(n)
+        return carry
+
+    lax.fori_loop(0, 2, tick_body, 0)
+    y_copy(pieces).wait_recv()
+    for i in range(4):
+        normalise(pl.multiple_of(other * half + i * (half // 4), half // 4), half // 4)
+    score(CHUNKS, own_keys, True)
+    lax.fori_loop(2, CHUNKS + 3, tick_body, 0)
+
+    top = jnp.max(peak[...], 0, keepdims=True)
+    share = jnp.sum(total[...] * jnp.exp2(peak[...] - top), 0, keepdims=True)
+    mine = top + LOG2E * jnp.log(share)
+    for h in range(2):
+        ex[h] = mine[:, h * half : (h + 1) * half]
+        ex[2 + h] = spos[:, h * half : (h + 1) * half]
+
+    def lse_copy(j, h):
+        side = f if h == 0 else other
+        return remote(ex.at[side], rl.at[j, f], l_send.at[j, h], l_recv.at[j, f], (far[j], side))
+
+    def lse_arrival(j, side):
+        return remote(ex.at[0], rl.at[j, side], l_send.at[j, 0], l_recv.at[j, side], peer)
+
+    ex_copy = remote(ex, ex_in, e_send, e_recv, peer)
+    for j in range(GROUP - 1, -1, -1):
+        for h in range(2):
+            lse_copy(j, h).start()
+    ex_copy.start()
+
+    ex_copy.wait_recv()
+    for h in range(2):
+        lanes = slice(h * half, (h + 1) * half)
+        lse_own[:, lanes] = log2_add(ex[h], ex_in[h])
+        loss_ref[:, lanes] = LN2 * (lse_own[:, lanes] - (ex[2 + h] + ex_in[2 + h]))
+    lse_rows[...] = jnp.zeros_like(lse_rows)
+    lse_rows[pl.ds(GROUP, 1), :] = log2_add(ex[f], ex_in[f])
+    for j in range(GROUP):
+        for side in range(2):
+            lse_arrival(j, side).wait_recv()
+        lse_rows[pl.ds(j, 1), :] = log2_add(rl[j, 0], rl[j, 1])
+    columns = lse_rows[...].T
+    for j in range(GROUP):
+        spread = jnp.broadcast_to(columns[:, j : j + 1], (half, 128))
+        lse_keys[pl.ds(0, CHUNKS), j] = spread.reshape(CHUNKS, step_rows, 128)
+    lse_keys[CHUNKS] = jnp.broadcast_to(columns[:, GROUP : GROUP + 1], (half, 128)).reshape(
+        GROUP, step_rows, 128
+    )
+
+    tiles = rows // tile
+
+    def keys_of(c, h):
+        if c == CHUNKS:
+            return own_keys(h)
+        return kb[h, c].reshape(half, width)
+
+    def g_copy(i):
+        return remote(g_out.at[i], g_in.at[i], g_send.at[i], g_recv.at[i], peer)
+
+    def send_tile(i, carry):
+        lanes = pl.ds(pl.multiple_of(i * tile, tile), tile)
+        lse_query = lse_own[:, lanes]
+        acc = jnp.zeros((tile, width), jnp.float32)
+        inner = jnp.zeros((8, tile), jnp.float32)
+        for c in range(CHUNKS + 1):
+            block = st[i, c]
+            weight = jnp.exp2(block - lse_query) + jnp.exp2(block - lse_keys[c].reshape(half, 128))
+            if c == CHUNKS:
+                key_ids = lax.broadcasted_iota(jnp.int32, block.shape, 0) + f * half
+                weight = weight - jnp.where(key_ids == pos_ref[:, lanes], 2.0, 0.0)
+            rounded = weight.astype(jnp.bfloat16)
+            wt[i, c] = rounded
+            inner = inner + jnp.sum(
+                (rounded.astype(jnp.float32) * block).reshape(half // 8, 8, tile), 0
+            )
+            acc = acc + dot_tn(rounded, keys_of(c, other))
+        rad[:, lanes] = jnp.sum(inner, 0, keepdims=True)
+        g_out[i] = acc.astype(jnp.bfloat16)
+        g_copy(i).start()
+        return carry
+
+    lax.fori_loop(0, tiles, send_tile, 0)
+    rad_out[0] = rad[...]
+    rad_copy = remote(rad_out, rad_in, r_send, r_recv, peer)
+    rad_copy.start()
+
+    def keep_tile(i, carry):
+        acc = jnp.zeros((tile, width), jnp.float32)
+        for c in range(CHUNKS + 1):
+            acc = acc + dot_tn(wt[i, c], keys_of(c, f))
+        grad_ref[pl.ds(pl.multiple_of(i * tile, tile), tile), :] = acc
+        return carry
+
+    lax.fori_loop(0, tiles, keep_tile, 0)
+    rad_copy.wait_recv()
+    radial = jnp.broadcast_to(LN2 * (rad_out[0] + rad_in[0]), (128, rows)).T
+    sharpness = sharp_ref[0, 0]
+    for i in range(tiles):
+        spot = slice(i * tile, (i + 1) * tile)
+        g_copy(i).wait_recv()
+        inverse = inv[spot, :1]
+        unit = proj_ref[spot, :].astype(jnp.float32) * inverse
+        whole = (grad_ref[spot, :] + g_in[i].astype(jnp.float32)) * sharpness
+        grad_ref[spot, :] = inverse * (whole - unit * radial[spot, :1])
+
+    for i in range(pieces + 1):
+        y_copy(i).wait_send()
+    for slot in range(GROUP):
+        for c in range(CHUNKS):
+            send_key(slot, c).wait_send()
+    for j in range(GROUP):
+        for h in range(2):
+            lse_copy(j, h).wait_send()
+    ex_copy.wait_send()
+    rad_copy.wait_send()
+    for i in range(tiles):
+        g_copy(i).wait_send()
+
+
+def per_device(projected, sharpness, partners, positives):
+    rows, width = projected.shape
+    blocks = lax.axis_size("tour")
+    if blocks != 2 * GROUP or lax.axis_size("feat") != 2:
+        return per_device_any(projected, sharpness, partners, positives)
+    half = rows // 2
+    step_rows = half // CHUNKS
+    tiles = rows // 128
+    local_pos = (positives - lax.axis_index("tour") * rows)[None, :]
+    bf16, f32 = jnp.bfloat16, jnp.float32
+    dma = pltpu.SemaphoreType.DMA
+    loss, grad = pl.pallas_call(
+        functools.partial(kernel, GROUP, rows, width),
+        out_shape=(
+            jax.ShapeDtypeStruct((1, rows), f32),
+            jax.ShapeDtypeStruct((rows, width), f32),
+        ),
+        in_specs=[
+            pl.BlockSpec(memory_space=pltpu.SMEM),
+            pl.BlockSpec(memory_space=pltpu.VMEM),
+            pl.BlockSpec(memory_space=pltpu.VMEM),
+        ],
+        out_specs=[pl.BlockSpec(memory_space=pltpu.VMEM)] * 2,
+        scratch_shapes=[
+            pltpu.VMEM((2, rows, width), bf16),
+            pltpu.VMEM((2, rows, width), bf16),
+            pltpu.VMEM((rows, 128), f32),
+            pltpu.VMEM((2, CHUNKS, GROUP, step_rows, width), bf16),
+            pltpu.VMEM((tiles, CHUNKS + 1, half, 128), f32),
+            pltpu.VMEM((tiles, CHUNKS + 1, half, 128), bf16),
+            pltpu.VMEM((8, rows), f32),
+            pltpu.VMEM((8, rows), f32),
+            pltpu.VMEM((1, rows), f32),
+            pltpu.VMEM((1, rows), f32),
+            pltpu.VMEM((4, 1, half), f32),
+            pltpu.VMEM((4, 1, half), f32),
+            pltpu.VMEM((GROUP, 2, 1, half), f32),
+            pltpu.VMEM((128, half), f32),
+            pltpu.VMEM((CHUNKS + 1, GROUP, step_rows, 128), f32),
+            pltpu.VMEM((tiles, 128, width), bf16),
+            pltpu.VMEM((tiles, 128, width), bf16),
+            pltpu.VMEM((1, rows), f32),
+            pltpu.VMEM((1, 1, rows), f32),
+            pltpu.VMEM((1, 1, rows), f32),
+            dma((5,)), dma((5,)),
+            dma((GROUP, CHUNKS)), dma((GROUP, CHUNKS)),
+            dma((GROUP, 2)), dma((GROUP, 2)),
+            dma, dma,
+            dma((tiles,)), dma((tiles,)),
+            dma, dma,
+        ],
+        compiler_params=pltpu.CompilerParams(
+            collective_id=0, has_side_effects=True, vmem_limit_bytes=50 * 1024 * 1024
+        ),
+        cost_estimate=pl.CostEstimate(
+            flops=9 * 4 * rows * half * 2 * width, bytes_accessed=4 * rows * width,
+            transcendentals=27 * rows * half,
+        ),
+    )(sharpness.reshape(1, 1), projected, local_pos)
+    return loss[0], grad
+
+
 def solution(mesh):
     in_specs = (P("tour", "feat"), P(), P(), P("tour"))
     out_specs = (P("tour"), P("tour", "feat"))

time: 600 us -> 77.9 us (0.13)
  waiting for transfers between devices: 478 us -> 0 us
  Pallas kernels: 0 us -> 73.8 us
  between operations: 35.7 us -> 1.32 us
  starting transfers between devices: 33 us -> 0 us
  matrix products: 19 us -> 0 us
  other arithmetic: 11 us -> 0.01 us
  blocking collectives: 10.8 us -> 0 us
  local copies, waits for them, and re-layouts: 11.2 us -> 2.6 us
    ppermute x29 -> x0, waiting for transfers between devices: 256 us -> none  [from_partner(): return lax.ppermute(value, axis, pairs)]
    psum x1 -> x0, waiting for transfers between devices: 223 us -> none  [scored(): return lax.psum(similar(embedded, key_block), 'feat') * sharpness]
    pallas_call x0 -> x1, Pallas kernels: none -> 73.8 us  [per_device(): pl.pallas_call(functools.partial(kernel, GROUP, rows, width), out_shape=(...]
    ppermute x29 -> x0, starting transfers between devices: 32.9 us -> none  [from_partner(): return lax.ppermute(value, axis, pairs)]
    dot_general x18 -> x0, matrix products: 19 us -> none  [the longest x9 13.3 us: similar(): jnp.einsum('qd,kd->qk', queries, key_block, preferred_element_type=jnp.fl...]
    psum x2 -> x0, blocking collectives: 10.8 us -> none  [the longest x1 5.87 us: per_device(): lax.psum(jnp.sum(floats * floats, -1), 'feat') + EPSILON]
    unnamed x76 -> x6, local copies, waits for them, and re-layouts: 10 us -> 2.6 us
  transfers between devices with their start and end apart: 30 -> 0, of which waited for: 22 -> 0; matrix products, arithmetic and copies ran while one was open for 2% -> 0% of each run, Pallas kernels for 0% -> 0%
where the time goes in v1:
time: 77.9 us; the launch traced here: 77.7 us
  Pallas kernels  73.8 us (95%)
  local copies, waits for them, and re-layouts  2.6 us (3%)
  between operations  1.32 us (2%)
    pallas_call x1, Pallas kernels, per_device(): pl.pallas_call(functools.partial(kernel, GROUP, rows, width), out_shape=(...  73.8 us
    unnamed x6, local copies, waits for them, and re-layouts  2.6 us

profile of v1, /device:TPU:0, one launch (start us, length us, event | category | flops | bytes accessed | tf_op | source)
XLA Modules:
  0.0 77.7 jit_solution(5243458469083455266)
XLA Ops:
  0.6 0.0 copy-start.1
  1.3 0.0 copy-done.1
  1.3 0.0 copy-start
  1.3 1.0 %copy-done = bf16[512,512]{1,0:T(8,128)(2,1)S(1)} copy-done((bf16[512,512]{1,0:T(8,128)(2,1)S(1)}, bf16[512,512]{1,0:T(8,128)(2,1)}, u32[]{:S(2)}) %copy-start) | copy-done | bytes 524312
  2.4 73.8 %shard_map.50 = (f32[1,512]{1,0:T(1,128)S(1)}, f32[512,512]{1,0:T(8,128)S(1)}) custom-call(f32[1,1]{1,0:T(1,128)} %bitcast.3.sharp_ref, bf16[512,512]{1,0:T(8,128)(2,1)S(1)} %copy-done, s32[1,512]{1,0:T(1,128)S(1)} %bitcast.4), custom_call_target="tpu_custom_call" | custom-call | flops 4831838208 | bytes 1048576 | tf_op jit(solution)/shard_map/pallas_call | solution.py:395
  76.1 0.6 copy.8
  76.7 1.0 %copy.9 = f32[512,512]{1,0:T(8,128)} copy(f32[512,512]{1,0:T(8,128)S(1)} %get-tuple-element.9) | data formatting | bytes 2097152
  (1 shorter events, 0.0 us)
Async XLA Ops:
  0.6 0.7 copy-start.1
  1.3 1.0 %copy-start = (bf16[512,512]{1,0:T(8,128)(2,1)S(1)}, bf16[512,512]{1,0:T(8,128)(2,1)}, u32[]{:S(2)}) copy-start(bf16[512,512]{1,0:T(8,128)(2,1)} %proj_ref.1) | copy-start | bytes 1572868

commit v2 on v1

--- a/solution.py
+++ b/solution.py
@@ -103,6 +103,7 @@
 LN2 = math.log(2.0)
 GROUP = 8
 CHUNKS = 8
+WINDOW = 4
 FAR = -1e30
 
 
@@ -131,7 +132,7 @@
     mask, rows, width, sharp_ref, proj_ref, pos_ref, loss_ref, grad_ref,
     raw, q, inv, kb, st, wt, peak, total, spos, lse_own, ex, ex_in, rl, lse_rows, lse_keys,
     g_out, g_in, rad, rad_out, rad_in,
-    y_send, y_recv, k_send, k_recv, l_send, l_recv, e_send, e_recv, g_send, g_recv, r_send, r_recv,
+    own_sem, y_send, y_recv, k_send, k_recv, l_send, l_recv, e_send, e_recv, g_send, g_recv, r_send, r_recv,
 ):
     half = rows // 2
     step_rows = half // CHUNKS
@@ -159,15 +160,15 @@
     piece = half // pieces
 
     def y_copy(i):
-        if i < pieces:
-            spot = pl.ds(pl.multiple_of(other * half + i * piece, piece), piece)
-        else:
-            spot = pl.ds(pl.multiple_of(f * half, half), half)
+        side = other if i < pieces else f
+        spot = pl.ds(pl.multiple_of(side * half + (i % pieces) * piece, piece), piece)
         return remote(proj_ref.at[spot], raw.at[f, spot], y_send.at[i], y_recv.at[i], peer)
 
-    for i in range(pieces + 1):
+    for i in range(pieces):
         y_copy(i).start()
-    raw[f] = proj_ref[...]
+    own_copy = pltpu.make_async_copy(proj_ref, raw.at[f], own_sem)
+    own_copy.start()
+    own_copy.wait()
 
     def normalise(start, count):
         spot = pl.ds(start, count)
@@ -200,7 +201,9 @@
         y_copy(i).wait_recv()
         normalise(pl.multiple_of(f * half + i * piece, piece), piece)
         for c in range(i * CHUNKS // pieces, (i + 1) * CHUNKS // pieces):
-            cross(c).start()
+            if c < WINDOW:
+                cross(c).start()
+        y_copy(pieces + i).start()
 
     tile = 128
 
@@ -242,6 +245,10 @@
             for slot in (4, 2, 1):
                 send_key(slot, n).start()
 
+        @pl.when(n + WINDOW < CHUNKS)
+        def _():
+            cross(n + WINDOW).start()
+
         @pl.when((n >= 1) & (n < CHUNKS + 1))
         def _():
             send_key(4, n - 1).wait_recv()
@@ -266,9 +273,9 @@
         return carry
 
     lax.fori_loop(0, 2, tick_body, 0)
-    y_copy(pieces).wait_recv()
-    for i in range(4):
-        normalise(pl.multiple_of(other * half + i * (half // 4), half // 4), half // 4)
+    for i in range(pieces):
+        y_copy(pieces + i).wait_recv()
+        normalise(pl.multiple_of(other * half + i * piece, piece), piece)
     score(CHUNKS, own_keys, True)
     lax.fori_loop(2, CHUNKS + 3, tick_body, 0)
 
@@ -363,11 +370,11 @@
         spot = slice(i * tile, (i + 1) * tile)
         g_copy(i).wait_recv()
         inverse = inv[spot, :1]
-        unit = proj_ref[spot, :].astype(jnp.float32) * inverse
+        unit = raw[f, spot, :].astype(jnp.float32) * inverse
         whole = (grad_ref[spot, :] + g_in[i].astype(jnp.float32)) * sharpness
         grad_ref[spot, :] = inverse * (whole - unit * radial[spot, :1])
 
-    for i in range(pieces + 1):
+    for i in range(2 * pieces):
         y_copy(i).wait_send()
     for slot in range(GROUP):
         for c in range(CHUNKS):
@@ -400,7 +407,7 @@
         ),
         in_specs=[
             pl.BlockSpec(memory_space=pltpu.SMEM),
-            pl.BlockSpec(memory_space=pltpu.VMEM),
+            pl.BlockSpec(memory_space=pl.ANY),
             pl.BlockSpec(memory_space=pltpu.VMEM),
         ],
         out_specs=[pl.BlockSpec(memory_space=pltpu.VMEM)] * 2,
@@ -425,7 +432,7 @@
             pltpu.VMEM((1, rows), f32),
             pltpu.VMEM((1, 1, rows), f32),
             pltpu.VMEM((1, 1, rows), f32),
-            dma((5,)), dma((5,)),
+            dma, dma((8,)), dma((8,)),
             dma((GROUP, CHUNKS)), dma((GROUP, CHUNKS)),
             dma((GROUP, 2)), dma((GROUP, 2)),
             dma, dma,

time: 77.9 us -> 74 us (0.950)
  Pallas kernels: 73.8 us -> 69.9 us
    pallas_call x1, Pallas kernels: 73.8 us -> 69.9 us  [per_device(): pl.pallas_call(functools.partial(kernel, GROUP, rows, width), out_shape=(...]
where the time goes in v2:
time: 74 us; the launch traced here: 73.8 us
  Pallas kernels  69.9 us (94%)
  local copies, waits for them, and re-layouts  2.6 us (4%)
  between operations  1.32 us (2%)
    pallas_call x1, Pallas kernels, per_device(): pl.pallas_call(functools.partial(kernel, GROUP, rows, width), out_shape=(...  69.9 us
    unnamed x6, local copies, waits for them, and re-layouts  2.6 us

profile of v2, /device:TPU:0, one launch (start us, length us, event | category | flops | bytes accessed | tf_op | source)
XLA Modules:
  0.0 73.8 jit_solution(18186395743928146173)
XLA Ops:
  0.6 0.0 copy-start.1
  1.3 0.0 copy-done.1
  1.3 0.0 copy-start
  1.3 1.0 %copy-done = bf16[512,512]{1,0:T(8,128)(2,1)S(1)} copy-done((bf16[512,512]{1,0:T(8,128)(2,1)S(1)}, bf16[512,512]{1,0:T(8,128)(2,1)}, u32[]{:S(2)}) %copy-start) | copy-done | bytes 524312
  2.4 69.9 %shard_map.50 = (f32[1,512]{1,0:T(1,128)S(1)}, f32[512,512]{1,0:T(8,128)S(1)}) custom-call(f32[1,1]{1,0:T(1,128)} %bitcast.3.sharp_ref, bf16[512,512]{1,0:T(8,128)(2,1)S(1)} %copy-done, s32[1,512]{1,0:T(1,128)S(1)} %bitcast.4), custom_call_target="tpu_custom_call" | custom-call | flops 4831838208 | bytes 1048576 | tf_op jit(solution)/shard_map/pallas_call | solution.py:402
  72.3 0.6 copy.8
  72.8 1.0 %copy.9 = f32[512,512]{1,0:T(8,128)} copy(f32[512,512]{1,0:T(8,128)S(1)} %get-tuple-element.9) | data formatting | bytes 2097152
  (1 shorter events, 0.0 us)
Async XLA Ops:
  0.6 0.7 copy-start.1
  1.3 1.0 %copy-start = (bf16[512,512]{1,0:T(8,128)(2,1)S(1)}, bf16[512,512]{1,0:T(8,128)(2,1)}, u32[]{:S(2)}) copy-start(bf16[512,512]{1,0:T(8,128)(2,1)} %proj_ref.1) | copy-start | bytes 1572868

commit v3 on v2

--- a/solution.py
+++ b/solution.py
@@ -103,7 +103,9 @@
 LN2 = math.log(2.0)
 GROUP = 8
 CHUNKS = 8
+STEPS = 16
 WINDOW = 4
+LAGS = (2, 4, 5)
 FAR = -1e30
 
 
@@ -124,8 +126,8 @@
     return lax.dot_general(a, b, (((1,), (1,)), ((), ())), preferred_element_type=jnp.float32)
 
 
-def dot_tn(a, b):
-    return lax.dot_general(a, b, (((0,), (0,)), ((), ())), preferred_element_type=jnp.float32)
+def dot_nn(a, b):
+    return jnp.dot(a, b, preferred_element_type=jnp.float32)
 
 
 def kernel(
@@ -180,29 +182,36 @@
         q[1, spot, :] = (right * inverse).astype(jnp.bfloat16)
         inv[spot, :] = jnp.broadcast_to(inverse, (count, 128))
 
-    def cross(c):
-        spot = pl.ds(pl.multiple_of(f * half + c * step_rows, step_rows), step_rows)
-        return remote(q.at[:, spot], kb.at[:, c, 0], k_send.at[0, c], k_recv.at[0, c], (far[0], f))
-
-    def forward(src, dst, bit, c):
+    send_rows = half // STEPS
+    merged = STEPS // CHUNKS
+
+    def landing(slot, n):
+        spot = pl.ds(pl.multiple_of((n % merged) * send_rows, send_rows), send_rows)
+        return kb.at[:, n // merged, slot, spot]
+
+    def cross(n):
+        spot = pl.ds(pl.multiple_of(f * half + n * send_rows, send_rows), send_rows)
+        return remote(q.at[:, spot], landing(0, n), k_send.at[0, n], k_recv.at[0, n], (far[0], f))
+
+    def forward(src, dst, bit, n):
         return remote(
-            kb.at[:, c, src], kb.at[:, c, dst], k_send.at[dst, c], k_recv.at[dst, c], near[bit]
+            landing(src, n), landing(dst, n), k_send.at[dst, n], k_recv.at[dst, n], near[bit]
         )
 
     hops = {1: (0, 1), 2: (0, 2), 3: (2, 1), 4: (0, 4), 5: (4, 1), 6: (4, 2), 7: (6, 1)}
 
-    def send_key(slot, c):
+    def send_key(slot, n):
         if slot == 0:
-            return cross(c)
+            return cross(n)
         src, bit = hops[slot]
-        return forward(src, slot, bit, c)
+        return forward(src, slot, bit, n)
 
     for i in range(pieces):
         y_copy(i).wait_recv()
         normalise(pl.multiple_of(f * half + i * piece, piece), piece)
-        for c in range(i * CHUNKS // pieces, (i + 1) * CHUNKS // pieces):
-            if c < WINDOW:
-                cross(c).start()
+        for n in range(i * STEPS // pieces, (i + 1) * STEPS // pieces):
+            if n < WINDOW:
+                cross(n).start()
         y_copy(pieces + i).start()
 
     tile = 128
@@ -239,45 +248,51 @@
         return lambda h: kb[h, c].reshape(half, width)
 
     def tick(n):
-        @pl.when(n < CHUNKS)
+        one, two, three = (n - lag for lag in LAGS)
+
+        @pl.when(n < STEPS)
         def _():
             send_key(0, n).wait_recv()
+
+            @pl.when(n + WINDOW < STEPS)
+            def _():
+                cross(n + WINDOW).start()
+
             for slot in (4, 2, 1):
                 send_key(slot, n).start()
 
-        @pl.when(n + WINDOW < CHUNKS)
+        @pl.when((one >= 0) & (one < STEPS))
         def _():
-            cross(n + WINDOW).start()
-
-        @pl.when((n >= 1) & (n < CHUNKS + 1))
+            send_key(4, one).wait_recv()
+            send_key(6, one).start()
+            send_key(5, one).start()
+            send_key(2, one).wait_recv()
+            send_key(3, one).start()
+
+        @pl.when((two >= 0) & (two < STEPS))
         def _():
-            send_key(4, n - 1).wait_recv()
-            send_key(6, n - 1).start()
-            send_key(5, n - 1).start()
-            send_key(2, n - 1).wait_recv()
-            send_key(3, n - 1).start()
-
-        @pl.when((n >= 2) & (n < CHUNKS + 2))
-        def _():
-            send_key(6, n - 2).wait_recv()
-            send_key(7, n - 2).start()
-
-        @pl.when(n >= 3)
+            send_key(6, two).wait_recv()
+            send_key(7, two).start()
+
+        @pl.when(three >= 0)
         def _():
             for slot in (1, 3, 5, 7):
-                send_key(slot, n - 3).wait_recv()
-            score(n - 3, chunk_keys(n - 3), False)
+                send_key(slot, three).wait_recv()
+
+            @pl.when(three % merged == merged - 1)
+            def _():
+                score(three // merged, chunk_keys(three // merged), False)
 
     def tick_body(n, carry):
         tick(n)
         return carry
 
-    lax.fori_loop(0, 2, tick_body, 0)
+    lax.fori_loop(0, 3, tick_body, 0)
     for i in range(pieces):
         y_copy(pieces + i).wait_recv()
         normalise(pl.multiple_of(other * half + i * piece, piece), piece)
     score(CHUNKS, own_keys, True)
-    lax.fori_loop(2, CHUNKS + 3, tick_body, 0)
+    lax.fori_loop(3, STEPS + LAGS[2], tick_body, 0)
 
     top = jnp.max(peak[...], 0, keepdims=True)
     share = jnp.sum(total[...] * jnp.exp2(peak[...] - top), 0, keepdims=True)
@@ -340,11 +355,12 @@
                 key_ids = lax.broadcasted_iota(jnp.int32, block.shape, 0) + f * half
                 weight = weight - jnp.where(key_ids == pos_ref[:, lanes], 2.0, 0.0)
             rounded = weight.astype(jnp.bfloat16)
-            wt[i, c] = rounded
+            turned = rounded.T
+            wt[i, c] = turned
             inner = inner + jnp.sum(
                 (rounded.astype(jnp.float32) * block).reshape(half // 8, 8, tile), 0
             )
-            acc = acc + dot_tn(rounded, keys_of(c, other))
+            acc = acc + dot_nn(turned, keys_of(c, other))
         rad[:, lanes] = jnp.sum(inner, 0, keepdims=True)
         g_out[i] = acc.astype(jnp.bfloat16)
         g_copy(i).start()
@@ -358,7 +374,7 @@
     def keep_tile(i, carry):
         acc = jnp.zeros((tile, width), jnp.float32)
         for c in range(CHUNKS + 1):
-            acc = acc + dot_tn(wt[i, c], keys_of(c, f))
+            acc = acc + dot_nn(wt[i, c], keys_of(c, f))
         grad_ref[pl.ds(pl.multiple_of(i * tile, tile), tile), :] = acc
         return carry
 
@@ -377,8 +393,8 @@
     for i in range(2 * pieces):
         y_copy(i).wait_send()
     for slot in range(GROUP):
-        for c in range(CHUNKS):
-            send_key(slot, c).wait_send()
+        for n in range(STEPS):
+            send_key(slot, n).wait_send()
     for j in range(GROUP):
         for h in range(2):
             lse_copy(j, h).wait_send()
@@ -407,7 +423,7 @@
         ),
         in_specs=[
             pl.BlockSpec(memory_space=pltpu.SMEM),
-            pl.BlockSpec(memory_space=pl.ANY),
+            pl.BlockSpec(memory_space=pltpu.HBM),
             pl.BlockSpec(memory_space=pltpu.VMEM),
         ],
         out_specs=[pl.BlockSpec(memory_space=pltpu.VMEM)] * 2,
@@ -417,7 +433,7 @@
             pltpu.VMEM((rows, 128), f32),
             pltpu.VMEM((2, CHUNKS, GROUP, step_rows, width), bf16),
             pltpu.VMEM((tiles, CHUNKS + 1, half, 128), f32),
-            pltpu.VMEM((tiles, CHUNKS + 1, half, 128), bf16),
+            pltpu.VMEM((tiles, CHUNKS + 1, 128, half), bf16),
             pltpu.VMEM((8, rows), f32),
             pltpu.VMEM((8, rows), f32),
             pltpu.VMEM((1, rows), f32),
@@ -433,14 +449,14 @@
             pltpu.VMEM((1, 1, rows), f32),
             pltpu.VMEM((1, 1, rows), f32),
             dma, dma((8,)), dma((8,)),
-            dma((GROUP, CHUNKS)), dma((GROUP, CHUNKS)),
+            dma((GROUP, STEPS)), dma((GROUP, STEPS)),
             dma((GROUP, 2)), dma((GROUP, 2)),
             dma, dma,
             dma((tiles,)), dma((tiles,)),
             dma, dma,
         ],
         compiler_params=pltpu.CompilerParams(
-            collective_id=0, has_side_effects=True, vmem_limit_bytes=50 * 1024 * 1024
+            collective_id=0, has_side_effects=True, vmem_limit_bytes=63 * 1024 * 1024
         ),
         cost_estimate=pl.CostEstimate(
             flops=9 * 4 * rows * half * 2 * width, bytes_accessed=4 * rows * width,

time: 74 us -> 75.1 us (1.015)
  local copies, waits for them, and re-layouts: 2.6 us -> 3.51 us
    unnamed x6, local copies, waits for them, and re-layouts: 2.6 us -> 3.51 us
where the time goes in v3:
time: 75.1 us; the launch traced here: 74.9 us
  Pallas kernels  69.5 us (93%)
  local copies, waits for them, and re-layouts  3.51 us (5%)
  between operations  1.32 us (2%)
    pallas_call x1, Pallas kernels, per_device(): pl.pallas_call(functools.partial(kernel, GROUP, rows, width), out_shape=(...  69.5 us
    unnamed x6, local copies, waits for them, and re-layouts  3.51 us

profile of v3, /device:TPU:0, one launch (start us, length us, event | category | flops | bytes accessed | tf_op | source)
XLA Modules:
  0.0 74.9 jit_solution(15245707735718099184)
XLA Ops:
  0.6 0.0 copy-start
  1.3 0.0 copy-done
  1.3 0.6 broadcast_subtract_fusion
  1.9 69.5 %shard_map.50 = (f32[1,512]{1,0:T(1,128)}, f32[512,512]{1,0:T(8,128)}) custom-call(f32[1,1]{1,0:T(1,128)} %bitcast.3.sharp_ref, bf16[512,512]{1,0:T(8,128)(2,1)} %proj_ref.1, s32[1,512]{1,0:T(1,128)} %bitcast.4), custom_call_target="tpu_custom_call" | custom-call | flops 4831838208 | bytes 1048576 | tf_op jit(solution)/shard_map/pallas_call | solution.py:418
  71.4 0.0 copy-start.1
  71.4 0.7 copy-done.1
  72.0 0.6 copy.8
  72.6 2.3 %copy.9 = f32[512,512]{1,0:T(8,128)} copy(f32[512,512]{1,0:T(8,128)} %get-tuple-element.9) | data formatting | bytes 2097152
Async XLA Ops:
  0.6 0.7 copy-start
  71.4 0.7 copy-start.1

commit v4 on v3

--- a/solution.py
+++ b/solution.py
@@ -122,17 +122,13 @@
     return jnp.maximum(a, b) + LOG2E * jnp.log(1.0 + jnp.exp2(-jnp.abs(a - b)))
 
 
-def dot_nt(a, b):
-    return lax.dot_general(a, b, (((1,), (1,)), ((), ())), preferred_element_type=jnp.float32)
-
-
-def dot_nn(a, b):
+def dot(a, b):
     return jnp.dot(a, b, preferred_element_type=jnp.float32)
 
 
 def kernel(
     mask, rows, width, sharp_ref, proj_ref, pos_ref, loss_ref, grad_ref,
-    raw, q, inv, kb, st, wt, peak, total, spos, lse_own, ex, ex_in, rl, lse_rows, lse_keys,
+    raw, q, turned, inv, keys, st, wt, peak, total, spos, lse_own, ex, ex_in, rl, lse_rows, lse_keys,
     g_out, g_in, rad, rad_out, rad_in,
     own_sem, y_send, y_recv, k_send, k_recv, l_send, l_recv, e_send, e_recv, g_send, g_recv, r_send, r_recv,
 ):
@@ -178,20 +174,20 @@
         right = raw[1, spot, :].astype(jnp.float32)
         squares = jnp.sum(left * left, -1, keepdims=True) + jnp.sum(right * right, -1, keepdims=True)
         inverse = lax.rsqrt(squares + EPSILON)
-        q[0, spot, :] = (left * inverse).astype(jnp.bfloat16)
-        q[1, spot, :] = (right * inverse).astype(jnp.bfloat16)
+        q[spot, :width] = (left * inverse).astype(jnp.bfloat16)
+        q[spot, width:] = (right * inverse).astype(jnp.bfloat16)
         inv[spot, :] = jnp.broadcast_to(inverse, (count, 128))
 
     send_rows = half // STEPS
     merged = STEPS // CHUNKS
 
     def landing(slot, n):
-        spot = pl.ds(pl.multiple_of((n % merged) * send_rows, send_rows), send_rows)
-        return kb.at[:, n // merged, slot, spot]
+        start = (n // merged) * half + slot * step_rows + (n % merged) * send_rows
+        return keys.at[pl.ds(pl.multiple_of(start, send_rows), send_rows)]
 
     def cross(n):
         spot = pl.ds(pl.multiple_of(f * half + n * send_rows, send_rows), send_rows)
-        return remote(q.at[:, spot], landing(0, n), k_send.at[0, n], k_recv.at[0, n], (far[0], f))
+        return remote(q.at[spot], landing(0, n), k_send.at[0, n], k_recv.at[0, n], (far[0], f))
 
     def forward(src, dst, bit, n):
         return remote(
@@ -216,10 +212,11 @@
 
     tile = 128
 
-    def score(c, keys, own):
+    def score(c, own):
         for part in range(rows // 256):
             lanes = slice(part * 256, part * 256 + 256)
-            block = (dot_nt(keys(0), q[0, lanes, :]) + dot_nt(keys(1), q[1, lanes, :])) * scale
+            chunk = keys[pl.ds(pl.multiple_of(c * half, half), half), :]
+            block = dot(chunk, turned[:, lanes]) * scale
             if own:
                 key_ids = lax.broadcasted_iota(jnp.int32, block.shape, 0) + f * half
                 query_ids = lax.broadcasted_iota(jnp.int32, block.shape, 1) + part * 256
@@ -241,12 +238,6 @@
                     jnp.exp2(folded - top[None]), 0
                 )
 
-    def own_keys(h):
-        return q[h, pl.ds(pl.multiple_of(f * half, half), half), :]
-
-    def chunk_keys(c):
-        return lambda h: kb[h, c].reshape(half, width)
-
     def tick(n):
         one, two, three = (n - lag for lag in LAGS)
 
@@ -281,7 +272,7 @@
 
             @pl.when(three % merged == merged - 1)
             def _():
-                score(three // merged, chunk_keys(three // merged), False)
+                score(three // merged, False)
 
     def tick_body(n, carry):
         tick(n)
@@ -291,7 +282,9 @@
     for i in range(pieces):
         y_copy(pieces + i).wait_recv()
         normalise(pl.multiple_of(other * half + i * piece, piece), piece)
-    score(CHUNKS, own_keys, True)
+    turned[...] = q[...].T
+    keys[pl.ds(CHUNKS * half, half), :] = q[pl.ds(pl.multiple_of(f * half, half), half), :]
+    score(CHUNKS, True)
     lax.fori_loop(3, STEPS + LAGS[2], tick_body, 0)
 
     top = jnp.max(peak[...], 0, keepdims=True)
@@ -335,10 +328,8 @@
 
     tiles = rows // tile
 
-    def keys_of(c, h):
-        if c == CHUNKS:
-            return own_keys(h)
-        return kb[h, c].reshape(half, width)
+    def side_keys(side):
+        return keys[:, pl.ds(pl.multiple_of(side * width, width), width)]
 
     def g_copy(i):
         return remote(g_out.at[i], g_in.at[i], g_send.at[i], g_recv.at[i], peer)
@@ -346,7 +337,6 @@
     def send_tile(i, carry):
         lanes = pl.ds(pl.multiple_of(i * tile, tile), tile)
         lse_query = lse_own[:, lanes]
-        acc = jnp.zeros((tile, width), jnp.float32)
         inner = jnp.zeros((8, tile), jnp.float32)
         for c in range(CHUNKS + 1):
             block = st[i, c]
@@ -355,14 +345,12 @@
                 key_ids = lax.broadcasted_iota(jnp.int32, block.shape, 0) + f * half
                 weight = weight - jnp.where(key_ids == pos_ref[:, lanes], 2.0, 0.0)
             rounded = weight.astype(jnp.bfloat16)
-            turned = rounded.T
-            wt[i, c] = turned
+            wt[i, :, c * half : (c + 1) * half] = rounded.T
             inner = inner + jnp.sum(
                 (rounded.astype(jnp.float32) * block).reshape(half // 8, 8, tile), 0
             )
-            acc = acc + dot_nn(turned, keys_of(c, other))
         rad[:, lanes] = jnp.sum(inner, 0, keepdims=True)
-        g_out[i] = acc.astype(jnp.bfloat16)
+        g_out[i] = dot(wt[i], side_keys(other)).astype(jnp.bfloat16)
         g_copy(i).start()
         return carry
 
@@ -371,14 +359,13 @@
     rad_copy = remote(rad_out, rad_in, r_send, r_recv, peer)
     rad_copy.start()
 
-    def keep_tile(i, carry):
-        acc = jnp.zeros((tile, width), jnp.float32)
-        for c in range(CHUNKS + 1):
-            acc = acc + dot_nn(wt[i, c], keys_of(c, f))
-        grad_ref[pl.ds(pl.multiple_of(i * tile, tile), tile), :] = acc
+    def keep_tiles(i, carry):
+        weights = wt[pl.ds(2 * i, 2)].reshape(2 * tile, wt.shape[-1])
+        spot = pl.ds(pl.multiple_of(i * 2 * tile, 2 * tile), 2 * tile)
+        grad_ref[spot, :] = dot(weights, side_keys(f))
         return carry
 
-    lax.fori_loop(0, tiles, keep_tile, 0)
+    lax.fori_loop(0, tiles // 2, keep_tiles, 0)
     rad_copy.wait_recv()
     radial = jnp.broadcast_to(LN2 * (rad_out[0] + rad_in[0]), (128, rows)).T
     sharpness = sharp_ref[0, 0]
@@ -423,17 +410,18 @@
         ),
         in_specs=[
             pl.BlockSpec(memory_space=pltpu.SMEM),
-            pl.BlockSpec(memory_space=pltpu.HBM),
+            pl.BlockSpec(memory_space=pl.ANY),
             pl.BlockSpec(memory_space=pltpu.VMEM),
         ],
         out_specs=[pl.BlockSpec(memory_space=pltpu.VMEM)] * 2,
         scratch_shapes=[
             pltpu.VMEM((2, rows, width), bf16),
-            pltpu.VMEM((2, rows, width), bf16),
+            pltpu.VMEM((rows, 2 * width), bf16),
+            pltpu.VMEM((2 * width, rows), bf16),
             pltpu.VMEM((rows, 128), f32),
-            pltpu.VMEM((2, CHUNKS, GROUP, step_rows, width), bf16),
+            pltpu.VMEM(((CHUNKS + 1) * half, 2 * width), bf16),
             pltpu.VMEM((tiles, CHUNKS + 1, half, 128), f32),
-            pltpu.VMEM((tiles, CHUNKS + 1, 128, half), bf16),
+            pltpu.VMEM((tiles, 128, (CHUNKS + 1) * half), bf16),
             pltpu.VMEM((8, rows), f32),
             pltpu.VMEM((8, rows), f32),
             pltpu.VMEM((1, rows), f32),
@@ -456,7 +444,7 @@
             dma, dma,
         ],
         compiler_params=pltpu.CompilerParams(
-            collective_id=0, has_side_effects=True, vmem_limit_bytes=63 * 1024 * 1024
+            collective_id=0, has_side_effects=True, vmem_limit_bytes=50 * 1024 * 1024
         ),
         cost_estimate=pl.CostEstimate(
             flops=9 * 4 * rows * half * 2 * width, bytes_accessed=4 * rows * width,

time: 75.1 us -> 71.8 us (0.956)
  Pallas kernels: 69.5 us -> 67.7 us
  local copies, waits for them, and re-layouts: 3.51 us -> 2.6 us
    pallas_call x1, Pallas kernels: 69.5 us -> 67.7 us  [per_device(): pl.pallas_call(functools.partial(kernel, GROUP, rows, width), out_shape=(...]
    unnamed x6, local copies, waits for them, and re-layouts: 3.51 us -> 2.6 us
where the time goes in v4:
time: 71.8 us; the launch traced here: 71.7 us
  Pallas kernels  67.7 us (94%)
  local copies, waits for them, and re-layouts  2.6 us (4%)
  between operations  1.32 us (2%)
    pallas_call x1, Pallas kernels, per_device(): pl.pallas_call(functools.partial(kernel, GROUP, rows, width), out_shape=(...  67.7 us
    unnamed x6, local copies, waits for them, and re-layouts  2.6 us

profile of v4, /device:TPU:0, one launch (start us, length us, event | category | flops | bytes accessed | tf_op | source)
XLA Modules:
  0.0 71.7 jit_solution(15316649606875529971)
XLA Ops:
  0.6 0.0 copy-start.1
  1.3 0.0 copy-done.1
  1.3 0.0 copy-start
  1.3 1.0 %copy-done = bf16[512,512]{1,0:T(8,128)(2,1)S(1)} copy-done((bf16[512,512]{1,0:T(8,128)(2,1)S(1)}, bf16[512,512]{1,0:T(8,128)(2,1)}, u32[]{:S(2)}) %copy-start) | copy-done | bytes 524312
  2.4 67.7 %shard_map.50 = (f32[1,512]{1,0:T(1,128)S(1)}, f32[512,512]{1,0:T(8,128)S(1)}) custom-call(f32[1,1]{1,0:T(1,128)} %bitcast.3.sharp_ref, bf16[512,512]{1,0:T(8,128)(2,1)S(1)} %copy-done, s32[1,512]{1,0:T(1,128)S(1)} %bitcast.4), custom_call_target="tpu_custom_call" | custom-call | flops 4831838208 | bytes 1048576 | tf_op jit(solution)/shard_map/pallas_call | solution.py:405
  70.1 0.6 copy.8
  70.7 1.0 %copy.9 = f32[512,512]{1,0:T(8,128)} copy(f32[512,512]{1,0:T(8,128)S(1)} %get-tuple-element.9) | data formatting | bytes 2097152
  (1 shorter events, 0.0 us)
Async XLA Ops:
  0.6 0.7 copy-start.1
  1.3 1.0 %copy-start = (bf16[512,512]{1,0:T(8,128)(2,1)S(1)}, bf16[512,512]{1,0:T(8,128)(2,1)}, u32[]{:S(2)}) copy-start(bf16[512,512]{1,0:T(8,128)(2,1)} %proj_ref.1) | copy-start | bytes 1572868

commit v5 on v4

--- a/solution.py
+++ b/solution.py
@@ -104,8 +104,8 @@
 GROUP = 8
 CHUNKS = 8
 STEPS = 16
-WINDOW = 4
-LAGS = (2, 4, 5)
+WINDOW = 6
+LAGS = (3, 5, 8)
 FAR = -1e30
 
 
@@ -255,9 +255,18 @@
         @pl.when((one >= 0) & (one < STEPS))
         def _():
             send_key(4, one).wait_recv()
-            send_key(6, one).start()
+
+            @pl.when(one % 2 == 0)
+            def _():
+                forward(4, 6, 2, one).start()
+
             send_key(5, one).start()
             send_key(2, one).wait_recv()
+
+            @pl.when(one % 2 == 1)
+            def _():
+                forward(2, 6, 4, one).start()
+
             send_key(3, one).start()
 
         @pl.when((two >= 0) & (two < STEPS))
@@ -403,7 +412,7 @@
     bf16, f32 = jnp.bfloat16, jnp.float32
     dma = pltpu.SemaphoreType.DMA
     loss, grad = pl.pallas_call(
-        functools.partial(kernel, GROUP, rows, width),
+        functools.partial(kernel, GROUP + GROUP // 2, rows, width),
         out_shape=(
             jax.ShapeDtypeStruct((1, rows), f32),
             jax.ShapeDtypeStruct((rows, width), f32),

time: 71.8 us -> 73.9 us (1.029)
  Pallas kernels: 67.7 us -> 69.8 us
    pallas_call x1, Pallas kernels: 67.7 us -> 69.8 us  [per_device(): pl.pallas_call(functools.partial(kernel, GROUP + GROUP // 2, rows, width)...]
where the time goes in v5:
time: 73.9 us; the launch traced here: 73.7 us
  Pallas kernels  69.8 us (94%)
  local copies, waits for them, and re-layouts  2.6 us (4%)
  between operations  1.32 us (2%)
    pallas_call x1, Pallas kernels, per_device(): pl.pallas_call(functools.partial(kernel, GROUP + GROUP // 2, rows, width)...  69.8 us
    unnamed x6, local copies, waits for them, and re-layouts  2.6 us

profile of v5, /device:TPU:0, one launch (start us, length us, event | category | flops | bytes accessed | tf_op | source)
XLA Modules:
  0.0 73.7 jit_solution(12430949911987532451)
XLA Ops:
  0.6 0.0 copy-start.1
  1.3 0.0 copy-done.1
  1.3 0.0 copy-start
  1.3 1.0 %copy-done = bf16[512,512]{1,0:T(8,128)(2,1)S(1)} copy-done((bf16[512,512]{1,0:T(8,128)(2,1)S(1)}, bf16[512,512]{1,0:T(8,128)(2,1)}, u32[]{:S(2)}) %copy-start) | copy-done | bytes 524312
  2.4 69.8 %shard_map.50 = (f32[1,512]{1,0:T(1,128)S(1)}, f32[512,512]{1,0:T(8,128)S(1)}) custom-call(f32[1,1]{1,0:T(1,128)} %bitcast.3.sharp_ref, bf16[512,512]{1,0:T(8,128)(2,1)S(1)} %copy-done, s32[1,512]{1,0:T(1,128)S(1)} %bitcast.4), custom_call_target="tpu_custom_call" | custom-call | flops 4831838208 | bytes 1048576 | tf_op jit(solution)/shard_map/pallas_call | solution.py:414
  72.2 0.6 copy.8
  72.8 1.0 %copy.9 = f32[512,512]{1,0:T(8,128)} copy(f32[512,512]{1,0:T(8,128)S(1)} %get-tuple-element.9) | data formatting | bytes 2097152
  (1 shorter events, 0.0 us)
Async XLA Ops:
  0.6 0.7 copy-start.1
  1.3 1.0 %copy-start = (bf16[512,512]{1,0:T(8,128)(2,1)S(1)}, bf16[512,512]{1,0:T(8,128)(2,1)}, u32[]{:S(2)}) copy-start(bf16[512,512]{1,0:T(8,128)(2,1)} %proj_ref.1) | copy-start | bytes 1572868

commit v6 on v5

--- a/solution.py
+++ b/solution.py
@@ -1,5 +1,4 @@
 import functools
-import math
 from functools import reduce
 
 import jax
@@ -99,8 +98,6 @@
 
 
 MESH = pl.DeviceIdType.MESH
-LOG2E = math.log2(math.e)
-LN2 = math.log(2.0)
 GROUP = 8
 CHUNKS = 8
 STEPS = 16
@@ -118,8 +115,8 @@
     return index
 
 
-def log2_add(a, b):
-    return jnp.maximum(a, b) + LOG2E * jnp.log(1.0 + jnp.exp2(-jnp.abs(a - b)))
+def log_add(a, b):
+    return jnp.maximum(a, b) + jnp.log(1.0 + jnp.exp(-jnp.abs(a - b)))
 
 
 def dot(a, b):
@@ -140,7 +137,7 @@
     peer = (t, other)
     near = {bit: (flipped(t, bit), f) for bit in (1, 2, 4)}
     far = [flipped(t, mask ^ j) for j in range(GROUP)]
-    scale = sharp_ref[0, 0] * LOG2E
+    scale = sharp_ref[0, 0]
 
     barrier = pltpu.get_barrier_semaphore()
     everyone = [peer] + list(near.values()) + [(d, s) for d in far for s in (f, other)]
@@ -185,20 +182,22 @@
         start = (n // merged) * half + slot * step_rows + (n % merged) * send_rows
         return keys.at[pl.ds(pl.multiple_of(start, send_rows), send_rows)]
 
-    def cross(n):
+    def cross(n, slot=0):
         spot = pl.ds(pl.multiple_of(f * half + n * send_rows, send_rows), send_rows)
-        return remote(q.at[spot], landing(0, n), k_send.at[0, n], k_recv.at[0, n], (far[0], f))
+        return remote(
+            q.at[spot], landing(slot, n), k_send.at[slot, n], k_recv.at[slot, n], (far[slot], f)
+        )
 
     def forward(src, dst, bit, n):
         return remote(
             landing(src, n), landing(dst, n), k_send.at[dst, n], k_recv.at[dst, n], near[bit]
         )
 
-    hops = {1: (0, 1), 2: (0, 2), 3: (2, 1), 4: (0, 4), 5: (4, 1), 6: (4, 2), 7: (6, 1)}
+    hops = {2: (0, 2), 3: (2, 1), 4: (0, 4), 5: (4, 1), 6: (4, 2), 7: (6, 1)}
 
     def send_key(slot, n):
-        if slot == 0:
-            return cross(n)
+        if slot < 2:
+            return cross(n, slot)
         src, bit = hops[slot]
         return forward(src, slot, bit, n)
 
@@ -208,6 +207,7 @@
         for n in range(i * STEPS // pieces, (i + 1) * STEPS // pieces):
             if n < WINDOW:
                 cross(n).start()
+                cross(n, 1).start()
         y_copy(pieces + i).start()
 
     tile = 128
@@ -229,13 +229,13 @@
             top = jnp.max(folded, 0)
             if own:
                 peak[:, lanes] = top
-                total[:, lanes] = jnp.sum(jnp.exp2(folded - top[None]), 0)
+                total[:, lanes] = jnp.sum(jnp.exp(folded - top[None]), 0)
             else:
                 old = peak[:, lanes]
                 top = jnp.maximum(top, old)
                 peak[:, lanes] = top
-                total[:, lanes] = total[:, lanes] * jnp.exp2(old - top) + jnp.sum(
-                    jnp.exp2(folded - top[None]), 0
+                total[:, lanes] = total[:, lanes] * jnp.exp(old - top) + jnp.sum(
+                    jnp.exp(folded - top[None]), 0
                 )
 
     def tick(n):
@@ -248,9 +248,16 @@
             @pl.when(n + WINDOW < STEPS)
             def _():
                 cross(n + WINDOW).start()
-
-            for slot in (4, 2, 1):
+                cross(n + WINDOW, 1).start()
+
+            for slot in (4, 2):
                 send_key(slot, n).start()
+            send_key(1, n).wait_recv()
+
+            @pl.when(n % 4 == 0)
+            def _():
+                forward(1, 5, 4, n).start()
+                forward(1, 3, 2, n).start()
 
         @pl.when((one >= 0) & (one < STEPS))
         def _():
@@ -260,14 +267,19 @@
             def _():
                 forward(4, 6, 2, one).start()
 
-            send_key(5, one).start()
+            @pl.when(one % 4 > 0)
+            def _():
+                send_key(5, one).start()
+
             send_key(2, one).wait_recv()
 
             @pl.when(one % 2 == 1)
             def _():
                 forward(2, 6, 4, one).start()
 
-            send_key(3, one).start()
+            @pl.when(one % 4 > 0)
+            def _():
+                send_key(3, one).start()
 
         @pl.when((two >= 0) & (two < STEPS))
         def _():
@@ -276,7 +288,7 @@
 
         @pl.when(three >= 0)
         def _():
-            for slot in (1, 3, 5, 7):
+            for slot in (3, 5, 7):
                 send_key(slot, three).wait_recv()
 
             @pl.when(three % merged == merged - 1)
@@ -297,8 +309,8 @@
     lax.fori_loop(3, STEPS + LAGS[2], tick_body, 0)
 
     top = jnp.max(peak[...], 0, keepdims=True)
-    share = jnp.sum(total[...] * jnp.exp2(peak[...] - top), 0, keepdims=True)
-    mine = top + LOG2E * jnp.log(share)
+    share = jnp.sum(total[...] * jnp.exp(peak[...] - top), 0, keepdims=True)
+    mine = top + jnp.log(share)
     for h in range(2):
         ex[h] = mine[:, h * half : (h + 1) * half]
         ex[2 + h] = spos[:, h * half : (h + 1) * half]
@@ -319,14 +331,14 @@
     ex_copy.wait_recv()
     for h in range(2):
         lanes = slice(h * half, (h + 1) * half)
-        lse_own[:, lanes] = log2_add(ex[h], ex_in[h])
-        loss_ref[:, lanes] = LN2 * (lse_own[:, lanes] - (ex[2 + h] + ex_in[2 + h]))
+        lse_own[:, lanes] = log_add(ex[h], ex_in[h])
+        loss_ref[:, lanes] = lse_own[:, lanes] - (ex[2 + h] + ex_in[2 + h])
     lse_rows[...] = jnp.zeros_like(lse_rows)
-    lse_rows[pl.ds(GROUP, 1), :] = log2_add(ex[f], ex_in[f])
+    lse_rows[pl.ds(GROUP, 1), :] = log_add(ex[f], ex_in[f])
     for j in range(GROUP):
         for side in range(2):
             lse_arrival(j, side).wait_recv()
-        lse_rows[pl.ds(j, 1), :] = log2_add(rl[j, 0], rl[j, 1])
+        lse_rows[pl.ds(j, 1), :] = log_add(rl[j, 0], rl[j, 1])
     columns = lse_rows[...].T
     for j in range(GROUP):
         spread = jnp.broadcast_to(columns[:, j : j + 1], (half, 128))
@@ -349,7 +361,7 @@
         inner = jnp.zeros((8, tile), jnp.float32)
         for c in range(CHUNKS + 1):
             block = st[i, c]
-            weight = jnp.exp2(block - lse_query) + jnp.exp2(block - lse_keys[c].reshape(half, 128))
+            weight = jnp.exp(block - lse_query) + jnp.exp(block - lse_keys[c].reshape(half, 128))
             if c == CHUNKS:
                 key_ids = lax.broadcasted_iota(jnp.int32, block.shape, 0) + f * half
                 weight = weight - jnp.where(key_ids == pos_ref[:, lanes], 2.0, 0.0)
@@ -376,7 +388,7 @@
 
     lax.fori_loop(0, tiles // 2, keep_tiles, 0)
     rad_copy.wait_recv()
-    radial = jnp.broadcast_to(LN2 * (rad_out[0] + rad_in[0]), (128, rows)).T
+    radial = jnp.broadcast_to(rad_out[0] + rad_in[0], (128, rows)).T
     sharpness = sharp_ref[0, 0]
     for i in range(tiles):
         spot = slice(i * tile, (i + 1) * tile)

time: 73.9 us -> 91 us (1.23)
  Pallas kernels: 69.8 us -> 86.9 us
    pallas_call x1, Pallas kernels: 69.8 us -> 86.9 us  [per_device(): pl.pallas_call(functools.partial(kernel, GROUP + GROUP // 2, rows, width)...]
where the time goes in v6:
time: 91 us; the launch traced here: 90.8 us
  Pallas kernels  86.9 us (95%)
  local copies, waits for them, and re-layouts  2.6 us (3%)
  between operations  1.32 us (1%)
    pallas_call x1, Pallas kernels, per_device(): pl.pallas_call(functools.partial(kernel, GROUP + GROUP // 2, rows, width)...  86.9 us
    unnamed x6, local copies, waits for them, and re-layouts  2.6 us

profile of v6, /device:TPU:0, one launch (start us, length us, event | category | flops | bytes accessed | tf_op | source)
XLA Modules:
  0.0 90.8 jit_solution(16690526033879087606)
XLA Ops:
  0.6 0.0 copy-start.1
  1.3 0.0 copy-done.1
  1.3 0.0 copy-start
  1.3 1.0 %copy-done = bf16[512,512]{1,0:T(8,128)(2,1)S(1)} copy-done((bf16[512,512]{1,0:T(8,128)(2,1)S(1)}, bf16[512,512]{1,0:T(8,128)(2,1)}, u32[]{:S(2)}) %copy-start) | copy-done | bytes 524312
  2.4 86.9 %shard_map.50 = (f32[1,512]{1,0:T(1,128)S(1)}, f32[512,512]{1,0:T(8,128)S(1)}) custom-call(f32[1,1]{1,0:T(1,128)} %bitcast.3.sharp_ref, bf16[512,512]{1,0:T(8,128)(2,1)S(1)} %copy-done, s32[1,512]{1,0:T(1,128)S(1)} %bitcast.4), custom_call_target="tpu_custom_call" | custom-call | flops 4831838208 | bytes 1048576 | tf_op jit(solution)/shard_map/pallas_call | solution.py:426
  89.3 0.6 copy.8
  89.9 1.0 %copy.9 = f32[512,512]{1,0:T(8,128)} copy(f32[512,512]{1,0:T(8,128)S(1)} %get-tuple-element.9) | data formatting | bytes 2097152
  (1 shorter events, 0.0 us)
Async XLA Ops:
  0.6 0.7 copy-start.1
  1.3 1.0 %copy-start = (bf16[512,512]{1,0:T(8,128)(2,1)S(1)}, bf16[512,512]{1,0:T(8,128)(2,1)}, u32[]{:S(2)}) copy-start(bf16[512,512]{1,0:T(8,128)(2,1)} %proj_ref.1) | copy-start | bytes 1572868

commit v7 on v4

--- a/solution.py
+++ b/solution.py
@@ -1,5 +1,4 @@
 import functools
-import math
 from functools import reduce
 
 import jax
@@ -99,13 +98,11 @@
 
 
 MESH = pl.DeviceIdType.MESH
-LOG2E = math.log2(math.e)
-LN2 = math.log(2.0)
 GROUP = 8
 CHUNKS = 8
 STEPS = 16
-WINDOW = 4
-LAGS = (2, 4, 5)
+WINDOW = 6
+LAGS = (2, 4, 6)
 FAR = -1e30
 
 
@@ -118,8 +115,12 @@
     return index
 
 
-def log2_add(a, b):
-    return jnp.maximum(a, b) + LOG2E * jnp.log(1.0 + jnp.exp2(-jnp.abs(a - b)))
+def log_add(a, b):
+    return jnp.maximum(a, b) + jnp.log(1.0 + jnp.exp(-jnp.abs(a - b)))
+
+
+def dot_nt(a, b):
+    return lax.dot_general(a, b, (((1,), (1,)), ((), ())), preferred_element_type=jnp.float32)
 
 
 def dot(a, b):
@@ -128,7 +129,7 @@
 
 def kernel(
     mask, rows, width, sharp_ref, proj_ref, pos_ref, loss_ref, grad_ref,
-    raw, q, turned, inv, keys, st, wt, peak, total, spos, lse_own, ex, ex_in, rl, lse_rows, lse_keys,
+    raw, q, pos_col, lse_col, inv, keys, st, wt, peak, total, spos, lse_own, ex, ex_in, rl, lse_rows, lse_keys,
     g_out, g_in, rad, rad_out, rad_in,
     own_sem, y_send, y_recv, k_send, k_recv, l_send, l_recv, e_send, e_recv, g_send, g_recv, r_send, r_recv,
 ):
@@ -140,7 +141,7 @@
     peer = (t, other)
     near = {bit: (flipped(t, bit), f) for bit in (1, 2, 4)}
     far = [flipped(t, mask ^ j) for j in range(GROUP)]
-    scale = sharp_ref[0, 0] * LOG2E
+    scale = sharp_ref[0, 0]
 
     barrier = pltpu.get_barrier_semaphore()
     everyone = [peer] + list(near.values()) + [(d, s) for d in far for s in (f, other)]
@@ -211,31 +212,31 @@
         y_copy(pieces + i).start()
 
     tile = 128
+    pos_col[...] = jnp.broadcast_to(pos_ref[...], (128, rows)).T
 
     def score(c, own):
+        chunk = keys[pl.ds(pl.multiple_of(c * half, half), half), :]
         for part in range(rows // 256):
-            lanes = slice(part * 256, part * 256 + 256)
-            chunk = keys[pl.ds(pl.multiple_of(c * half, half), half), :]
-            block = dot(chunk, turned[:, lanes]) * scale
+            spot = slice(part * 256, part * 256 + 256)
+            block = dot_nt(q[spot, :], chunk) * scale
             if own:
-                key_ids = lax.broadcasted_iota(jnp.int32, block.shape, 0) + f * half
-                query_ids = lax.broadcasted_iota(jnp.int32, block.shape, 1) + part * 256
+                key_ids = lax.broadcasted_iota(jnp.int32, block.shape, 1) + f * half
+                query_ids = lax.broadcasted_iota(jnp.int32, block.shape, 0) + part * 256
                 block = jnp.where(key_ids == query_ids, FAR, block)
-                hit = key_ids == pos_ref[:, lanes]
-                spos[:, lanes] = jnp.sum(jnp.where(hit, block, 0.0), 0, keepdims=True)
-            for i in range(256 // tile):
-                st[part * (256 // tile) + i, c] = block[:, i * tile : (i + 1) * tile]
-            folded = block.reshape(half // 8, 8, 256)
-            top = jnp.max(folded, 0)
+                hits = jnp.where(key_ids == pos_col[spot, :1], block, 0.0)
+                spos[spot, :] = hits[:, :128] + hits[:, 128:]
+            st[c, spot, :] = block
+            left, right = block[:, :128], block[:, 128:]
+            top = jnp.maximum(left, right)
             if own:
-                peak[:, lanes] = top
-                total[:, lanes] = jnp.sum(jnp.exp2(folded - top[None]), 0)
+                peak[spot, :] = top
+                total[spot, :] = jnp.exp(left - top) + jnp.exp(right - top)
             else:
-                old = peak[:, lanes]
+                old = peak[spot, :]
                 top = jnp.maximum(top, old)
-                peak[:, lanes] = top
-                total[:, lanes] = total[:, lanes] * jnp.exp2(old - top) + jnp.sum(
-                    jnp.exp2(folded - top[None]), 0
+                peak[spot, :] = top
+                total[spot, :] = (
+                    total[spot, :] * jnp.exp(old - top) + jnp.exp(left - top) + jnp.exp(right - top)
                 )
 
     def tick(n):
@@ -282,17 +283,18 @@
     for i in range(pieces):
         y_copy(pieces + i).wait_recv()
         normalise(pl.multiple_of(other * half + i * piece, piece), piece)
-    turned[...] = q[...].T
     keys[pl.ds(CHUNKS * half, half), :] = q[pl.ds(pl.multiple_of(f * half, half), half), :]
     score(CHUNKS, True)
     lax.fori_loop(3, STEPS + LAGS[2], tick_body, 0)
 
-    top = jnp.max(peak[...], 0, keepdims=True)
-    share = jnp.sum(total[...] * jnp.exp2(peak[...] - top), 0, keepdims=True)
-    mine = top + LOG2E * jnp.log(share)
+    peaks = peak[...].T
+    top = jnp.max(peaks, 0, keepdims=True)
+    share = jnp.sum(total[...].T * jnp.exp(peaks - top), 0, keepdims=True)
+    mine = top + jnp.log(share)
+    paired = jnp.sum(spos[...].T, 0, keepdims=True)
     for h in range(2):
         ex[h] = mine[:, h * half : (h + 1) * half]
-        ex[2 + h] = spos[:, h * half : (h + 1) * half]
+        ex[2 + h] = paired[:, h * half : (h + 1) * half]
 
     def lse_copy(j, h):
         side = f if h == 0 else other
@@ -310,21 +312,25 @@
     ex_copy.wait_recv()
     for h in range(2):
         lanes = slice(h * half, (h + 1) * half)
-        lse_own[:, lanes] = log2_add(ex[h], ex_in[h])
-        loss_ref[:, lanes] = LN2 * (lse_own[:, lanes] - (ex[2 + h] + ex_in[2 + h]))
+        lse_own[:, lanes] = log_add(ex[h], ex_in[h])
+        loss_ref[:, lanes] = lse_own[:, lanes] - (ex[2 + h] + ex_in[2 + h])
     lse_rows[...] = jnp.zeros_like(lse_rows)
-    lse_rows[pl.ds(GROUP, 1), :] = log2_add(ex[f], ex_in[f])
+    lse_rows[pl.ds(GROUP, 1), :] = log_add(ex[f], ex_in[f])
     for j in range(GROUP):
         for side in range(2):
             lse_arrival(j, side).wait_recv()
-        lse_rows[pl.ds(j, 1), :] = log2_add(rl[j, 0], rl[j, 1])
+        lse_rows[pl.ds(j, 1), :] = log_add(rl[j, 0], rl[j, 1])
+    lse_col[...] = jnp.broadcast_to(lse_own[...], (128, rows)).T
     columns = lse_rows[...].T
+    lane_ids = lax.broadcasted_iota(jnp.int32, (step_rows, 128), 1)
+    parts = []
     for j in range(GROUP):
         spread = jnp.broadcast_to(columns[:, j : j + 1], (half, 128))
-        lse_keys[pl.ds(0, CHUNKS), j] = spread.reshape(CHUNKS, step_rows, 128)
-    lse_keys[CHUNKS] = jnp.broadcast_to(columns[:, GROUP : GROUP + 1], (half, 128)).reshape(
-        GROUP, step_rows, 128
-    )
+        part = jnp.zeros((step_rows, 128), jnp.float32)
+        for c in range(CHUNKS):
+            part = jnp.where(lane_ids == c, spread[c * step_rows : (c + 1) * step_rows], part)
+        parts.append(part)
+    lse_keys[...] = jnp.concatenate(parts, 0).T
 
     tiles = rows // tile
 
@@ -335,39 +341,39 @@
         return remote(g_out.at[i], g_in.at[i], g_send.at[i], g_recv.at[i], peer)
 
     def send_tile(i, carry):
-        lanes = pl.ds(pl.multiple_of(i * tile, tile), tile)
-        lse_query = lse_own[:, lanes]
-        inner = jnp.zeros((8, tile), jnp.float32)
+        spot = pl.ds(pl.multiple_of(i * tile, tile), tile)
+        lse_query = lse_col[spot, :]
+        inner = jnp.zeros((tile, 128), jnp.float32)
         for c in range(CHUNKS + 1):
-            block = st[i, c]
-            weight = jnp.exp2(block - lse_query) + jnp.exp2(block - lse_keys[c].reshape(half, 128))
-            if c == CHUNKS:
-                key_ids = lax.broadcasted_iota(jnp.int32, block.shape, 0) + f * half
-                weight = weight - jnp.where(key_ids == pos_ref[:, lanes], 2.0, 0.0)
-            rounded = weight.astype(jnp.bfloat16)
-            wt[i, :, c * half : (c + 1) * half] = rounded.T
-            inner = inner + jnp.sum(
-                (rounded.astype(jnp.float32) * block).reshape(half // 8, 8, tile), 0
-            )
-        rad[:, lanes] = jnp.sum(inner, 0, keepdims=True)
-        g_out[i] = dot(wt[i], side_keys(other)).astype(jnp.bfloat16)
+            row = lse_keys[c : c + 1, :] if c < CHUNKS else lse_rows[GROUP : GROUP + 1, :]
+            for h in range(half // 128):
+                lanes = slice(h * 128, (h + 1) * 128)
+                block = st[c, spot, lanes]
+                weight = jnp.exp(block - lse_query) + jnp.exp(block - row[:, lanes])
+                if c == CHUNKS:
+                    key_ids = lax.broadcasted_iota(jnp.int32, block.shape, 1) + f * half + h * 128
+                    weight = weight - jnp.where(key_ids == pos_col[spot, :], 2.0, 0.0)
+                rounded = weight.astype(jnp.bfloat16)
+                wt[spot, c * half + h * 128 : c * half + (h + 1) * 128] = rounded
+                inner = inner + rounded.astype(jnp.float32) * block
+        rad[spot, :] = inner
+        g_out[i] = dot(wt[spot, :], side_keys(other)).astype(jnp.bfloat16)
         g_copy(i).start()
         return carry
 
     lax.fori_loop(0, tiles, send_tile, 0)
-    rad_out[0] = rad[...]
+    rad_out[0] = jnp.sum(rad[...].T, 0, keepdims=True)
     rad_copy = remote(rad_out, rad_in, r_send, r_recv, peer)
     rad_copy.start()
 
     def keep_tiles(i, carry):
-        weights = wt[pl.ds(2 * i, 2)].reshape(2 * tile, wt.shape[-1])
         spot = pl.ds(pl.multiple_of(i * 2 * tile, 2 * tile), 2 * tile)
-        grad_ref[spot, :] = dot(weights, side_keys(f))
+        grad_ref[spot, :] = dot(wt[spot, :], side_keys(f))
         return carry
 
     lax.fori_loop(0, tiles // 2, keep_tiles, 0)
     rad_copy.wait_recv()
-    radial = jnp.broadcast_to(LN2 * (rad_out[0] + rad_in[0]), (128, rows)).T
+    radial = jnp.broadcast_to(rad_out[0] + rad_in[0], (128, rows)).T
     sharpness = sharp_ref[0, 0]
     for i in range(tiles):
         spot = slice(i * tile, (i + 1) * tile)
@@ -417,23 +423,24 @@
         scratch_shapes=[
             pltpu.VMEM((2, rows, width), bf16),
             pltpu.VMEM((rows, 2 * width), bf16),
-            pltpu.VMEM((2 * width, rows), bf16),
+            pltpu.VMEM((rows, 128), jnp.int32),
+            pltpu.VMEM((rows, 128), f32),
             pltpu.VMEM((rows, 128), f32),
             pltpu.VMEM(((CHUNKS + 1) * half, 2 * width), bf16),
-            pltpu.VMEM((tiles, CHUNKS + 1, half, 128), f32),
-            pltpu.VMEM((tiles, 128, (CHUNKS + 1) * half), bf16),
-            pltpu.VMEM((8, rows), f32),
-            pltpu.VMEM((8, rows), f32),
-            pltpu.VMEM((1, rows), f32),
+            pltpu.VMEM((CHUNKS + 1, rows, half), f32),
+            pltpu.VMEM((rows, (CHUNKS + 1) * half), bf16),
+            pltpu.VMEM((rows, 128), f32),
+            pltpu.VMEM((rows, 128), f32),
+            pltpu.VMEM((rows, 128), f32),
             pltpu.VMEM((1, rows), f32),
             pltpu.VMEM((4, 1, half), f32),
             pltpu.VMEM((4, 1, half), f32),
             pltpu.VMEM((GROUP, 2, 1, half), f32),
             pltpu.VMEM((128, half), f32),
-            pltpu.VMEM((CHUNKS + 1, GROUP, step_rows, 128), f32),
+            pltpu.VMEM((128, half), f32),
             pltpu.VMEM((tiles, 128, width), bf16),
             pltpu.VMEM((tiles, 128, width), bf16),
-            pltpu.VMEM((1, rows), f32),
+            pltpu.VMEM((rows, 128), f32),
             pltpu.VMEM((1, 1, rows), f32),
             pltpu.VMEM((1, 1, rows), f32),
             dma, dma((8,)), dma((8,)),

time: 71.8 us -> 73.8 us (1.028)
  Pallas kernels: 67.7 us -> 69.7 us
    pallas_call x1, Pallas kernels: 67.7 us -> 69.7 us  [per_device(): pl.pallas_call(functools.partial(kernel, GROUP, rows, width), out_shape=(...]
where the time goes in v7:
time: 73.8 us; the launch traced here: 73.6 us
  Pallas kernels  69.7 us (94%)
  local copies, waits for them, and re-layouts  2.6 us (4%)
  between operations  1.32 us (2%)
    pallas_call x1, Pallas kernels, per_device(): pl.pallas_call(functools.partial(kernel, GROUP, rows, width), out_shape=(...  69.7 us
    unnamed x6, local copies, waits for them, and re-layouts  2.6 us

profile of v7, /device:TPU:0, one launch (start us, length us, event | category | flops | bytes accessed | tf_op | source)
XLA Modules:
  0.0 73.6 jit_solution(12892294885374290119)
XLA Ops:
  0.6 0.0 copy-start.1
  1.3 0.0 copy-done.1
  1.3 0.0 copy-start
  1.3 1.0 %copy-done = bf16[512,512]{1,0:T(8,128)(2,1)S(1)} copy-done((bf16[512,512]{1,0:T(8,128)(2,1)S(1)}, bf16[512,512]{1,0:T(8,128)(2,1)}, u32[]{:S(2)}) %copy-start) | copy-done | bytes 524312
  2.4 69.7 %shard_map.50 = (f32[1,512]{1,0:T(1,128)S(1)}, f32[512,512]{1,0:T(8,128)S(1)}) custom-call(f32[1,1]{1,0:T(1,128)} %bitcast.3.sharp_ref, bf16[512,512]{1,0:T(8,128)(2,1)S(1)} %copy-done, s32[1,512]{1,0:T(1,128)S(1)} %bitcast.4), custom_call_target="tpu_custom_call" | custom-call | flops 4831838208 | bytes 1048576 | tf_op jit(solution)/shard_map/pallas_call | solution.py:411
  72.1 0.6 copy.8
  72.7 1.0 %copy.9 = f32[512,512]{1,0:T(8,128)} copy(f32[512,512]{1,0:T(8,128)S(1)} %get-tuple-element.9) | data formatting | bytes 2097152
  (1 shorter events, 0.0 us)
Async XLA Ops:
  0.6 0.7 copy-start.1
  1.3 1.0 %copy-start = (bf16[512,512]{1,0:T(8,128)(2,1)S(1)}, bf16[512,512]{1,0:T(8,128)(2,1)}, u32[]{:S(2)}) copy-start(bf16[512,512]{1,0:T(8,128)(2,1)} %proj_ref.1) | copy-start | bytes 1572868

commit v8 on v4

--- a/solution.py
+++ b/solution.py
@@ -104,8 +104,8 @@
 GROUP = 8
 CHUNKS = 8
 STEPS = 16
-WINDOW = 4
-LAGS = (2, 4, 5)
+WINDOW = 2
+LAGS = (2, 4, 6)
 FAR = -1e30
 
 
@@ -245,12 +245,12 @@
         def _():
             send_key(0, n).wait_recv()
 
+            for slot in (4, 2, 1):
+                send_key(slot, n).start()
+
             @pl.when(n + WINDOW < STEPS)
             def _():
                 cross(n + WINDOW).start()
-
-            for slot in (4, 2, 1):
-                send_key(slot, n).start()
 
         @pl.when((one >= 0) & (one < STEPS))
         def _():

time: 71.8 us -> 78 us (1.086)
  Pallas kernels: 67.7 us -> 73.8 us
    pallas_call x1, Pallas kernels: 67.7 us -> 73.8 us  [per_device(): pl.pallas_call(functools.partial(kernel, GROUP, rows, width), out_shape=(...]
where the time goes in v8:
time: 78 us; the launch traced here: 77.8 us
  Pallas kernels  73.8 us (95%)
  local copies, waits for them, and re-layouts  2.6 us (3%)
  between operations  1.32 us (2%)
    pallas_call x1, Pallas kernels, per_device(): pl.pallas_call(functools.partial(kernel, GROUP, rows, width), out_shape=(...  73.8 us
    unnamed x6, local copies, waits for them, and re-layouts  2.6 us

profile of v8, /device:TPU:0, one launch (start us, length us, event | category | flops | bytes accessed | tf_op | source)
XLA Modules:
  0.0 77.8 jit_solution(5990968435059260656)
XLA Ops:
  0.6 0.0 copy-start.1
  1.3 0.0 copy-done.1
  1.3 0.0 copy-start
  1.3 1.0 %copy-done = bf16[512,512]{1,0:T(8,128)(2,1)S(1)} copy-done((bf16[512,512]{1,0:T(8,128)(2,1)S(1)}, bf16[512,512]{1,0:T(8,128)(2,1)}, u32[]{:S(2)}) %copy-start) | copy-done | bytes 524312
  2.4 73.8 %shard_map.50 = (f32[1,512]{1,0:T(1,128)S(1)}, f32[512,512]{1,0:T(8,128)S(1)}) custom-call(f32[1,1]{1,0:T(1,128)} %bitcast.3.sharp_ref, bf16[512,512]{1,0:T(8,128)(2,1)S(1)} %copy-done, s32[1,512]{1,0:T(1,128)S(1)} %bitcast.4), custom_call_target="tpu_custom_call" | custom-call | flops 4831838208 | bytes 1048576 | tf_op jit(solution)/shard_map/pallas_call | solution.py:405
  76.2 0.6 copy.8
  76.8 1.0 %copy.9 = f32[512,512]{1,0:T(8,128)} copy(f32[512,512]{1,0:T(8,128)S(1)} %get-tuple-element.9) | data formatting | bytes 2097152
  (1 shorter events, 0.0 us)
Async XLA Ops:
  0.6 0.7 copy-start.1
  1.3 1.0 %copy-start = (bf16[512,512]{1,0:T(8,128)(2,1)S(1)}, bf16[512,512]{1,0:T(8,128)(2,1)}, u32[]{:S(2)}) copy-start(bf16[512,512]{1,0:T(8,128)(2,1)} %proj_ref.1) | copy-start | bytes 1572868
